TPU v7x, 128 devices: a whole 4x4x4 slice. The times are simulated.
128 devices in a mesh: seq: 16 (over z, x), pair: 8 (over y, core).
Axes of the slice: x: 4, y: 4, z: 4, core: 2. Of those that a mesh axis runs over, the one named last changes fastest.
Arguments:
- queries: bfloat16 [32768, 1024], P(('seq', 'pair')), may hold values from -6 to 6
- keys: bfloat16 [32768, 1024], P(('seq', 'pair')), may hold values from -6 to 6
- values: bfloat16 [32768, 1024], P(('seq', 'pair')), may hold values from -6 to 6
- out_grad: bfloat16 [32768, 1024], P(('seq', 'pair')), may hold values from -6 to 6
- event_bucket: int32 [32768], P(('seq', 'pair')), may hold values from 0 to 63
- slope: float32 [8], replicated, may hold values from 0.02 to 0.5
- block_user: int32 [128], replicated, may hold values from 0 to 31, as said below
- lengths: int32 [32], replicated, may hold values from 1 to 2048, as said below
Outputs:
- attn_out: bfloat16 [32768, 1024], P(('seq', 'pair'))
- grad_query: bfloat16 [32768, 1024], P(('seq', 'pair'))
- grad_key: bfloat16 [32768, 1024], P(('seq', 'pair'))
- grad_value: bfloat16 [32768, 1024], P(('seq', 'pair'))
Inputs may be any that keep to these rules, and one draw needn't show every extreme that they name: `block_user`: Nondecreasing; every user owns between 1 and 8 consecutive blocks, users in increasing order. A user owning c blocks has 256 * (c - 1) < lengths[u] <= 256 * c.
All inputs are finite; a program needn't handle non-finite values.
Results may differ from a plain program's by a relative error of at most 0.005.
Values may be sent and summed in bfloat16 or wider, within the bound.
A program may use at most 128 MiB of HBM per device.

v0:
```python
import jax
import jax.numpy as jnp
from jax import lax
from jax.sharding import PartitionSpec as P

BLK = 256
MAXB = 8


def shifted(value, axis, steps):
    count = lax.axis_size(axis)
    initial, last = (max(0, -steps), min(count, count - steps))
    return lax.ppermute(value, axis, [(source, source + steps) for source in range(initial, last)])


def event_info(block_index, block_user, lengths, block_span):
    block_count = block_user.shape[0]
    user_count = lengths.shape[0]
    inside = (block_index >= 0) & (block_index < block_count)
    matches = block_index[:, None] == jnp.arange(block_count, dtype=jnp.int32)[None, :]
    block_owner = jnp.sum(jnp.where(matches, block_user[None, :], 0), axis=1)
    first_block = jnp.sum((block_user[None, :] < block_owner[:, None]).astype(jnp.int32), axis=1)
    picked = jnp.arange(user_count, dtype=jnp.int32)[None, :] == block_owner[:, None]
    history = jnp.sum(jnp.where(picked, lengths[None, :], 0), axis=1)
    offsets = jnp.arange(block_span, dtype=jnp.int32)
    position = (block_index - first_block)[:, None] * block_span + offsets[None, :]
    usable = inside[:, None] & (position < history[:, None])
    global_event = block_index[:, None] * block_span + offsets[None, :]
    owner_rows = block_owner[:, None] + 0 * offsets[None, :]
    length_rows = history[:, None] + 0 * offsets[None, :]
    return (
        owner_rows.reshape(-1),
        usable.reshape(-1),
        global_event.reshape(-1),
        length_rows.reshape(-1),
    )


def per_device(queries, keys, values, out_grad, event_bucket, slope, block_user, lengths):
    row_count, full_width = queries.shape
    blocks_here = row_count // BLK
    head_count = slope.shape[0]
    head_dim = full_width // head_count
    score_scale = head_dim ** (-0.5)
    reach_blocks = (MAXB + blocks_here - 2) // blocks_here
    device = lax.axis_index(("seq", "pair"))
    own_parts = (keys, values, event_bucket.astype(jnp.bfloat16))
    pieces = [own_parts]
    for distance in range(1, reach_blocks + 1):
        pieces.append(
            shifted((own_parts[0], own_parts[1], own_parts[2]), ("seq", "pair"), distance)
        )
    window_keys, window_values, window_bucket = tuple(
        (jnp.concatenate([received[member] for received in pieces], axis=0) for member in range(3))
    )
    offsets = jnp.arange(blocks_here, dtype=jnp.int32)
    query_blocks = device * blocks_here + offsets
    distances = jnp.arange(reach_blocks + 1, dtype=jnp.int32)
    key_blocks = ((device - distances)[:, None] * blocks_here + offsets[None, :]).reshape(-1)
    q_owner, q_usable, q_global, q_length = event_info(query_blocks, block_user, lengths, BLK)
    k_owner, k_usable, k_global, k_length = event_info(key_blocks, block_user, lengths, BLK)
    visible = (
        q_usable[:, None]
        & k_usable[None, :]
        & (q_owner[:, None] == k_owner[None, :])
        & (k_global[None, :] <= q_global[:, None])
    )
    weight = jnp.where(visible, 1.0 / q_length.astype(jnp.float32)[:, None], jnp.float32(0.0))
    time_gap = jnp.abs(
        event_bucket.astype(jnp.float32)[:, None] - window_bucket.astype(jnp.float32)[None, :]
    )
    contract_last = (((1,), (1,)), ((), ()))
    contract_first = (((0,), (0,)), ((), ()))
    outputs, query_grads, key_grads, value_grads = ([], [], [], [])
    for head in range(head_count):
        lower = head * head_dim
        query_head = queries[:, lower : lower + head_dim]
        key_head = window_keys[:, lower : lower + head_dim]
        value_head = window_values[:, lower : lower + head_dim]
        grad_head = out_grad[:, lower : lower + head_dim]
        scores = (
            lax.dot_general(query_head, key_head, contract_last, preferred_element_type=jnp.float32)
            * score_scale
            - slope[head] * time_gap
        )
        squash = jax.nn.sigmoid(scores)
        attn = (scores * squash * weight).astype(jnp.bfloat16)
        outputs.append(jnp.dot(attn, value_head, preferred_element_type=jnp.float32))
        d_attn = lax.dot_general(
            grad_head, value_head, contract_last, preferred_element_type=jnp.float32
        )
        d_score = (d_attn * weight * (squash * (1.0 + scores * (1.0 - squash)))).astype(
            jnp.bfloat16
        )
        query_grads.append(
            jnp.dot(d_score, key_head, preferred_element_type=jnp.float32) * score_scale
        )
        key_grads.append(
            lax.dot_general(d_score, query_head, contract_first, preferred_element_type=jnp.float32)
            * score_scale
        )
        value_grads.append(
            lax.dot_general(attn, grad_head, contract_first, preferred_element_type=jnp.float32)
        )
    attn_out = jnp.concatenate(outputs, axis=1).astype(jnp.bfloat16)
    grad_query = jnp.concatenate(query_grads, axis=1).astype(jnp.bfloat16)
    partial_key = jnp.concatenate(key_grads, axis=1)
    partial_value = jnp.concatenate(value_grads, axis=1)
    summed_key = partial_key[:row_count]
    summed_value = partial_value[:row_count]
    for distance in range(1, reach_blocks + 1):
        lower = distance * row_count
        returned = shifted(
            (partial_key[lower : lower + row_count], partial_value[lower : lower + row_count]),
            ("seq", "pair"),
            -distance,
        )
        summed_key = summed_key + returned[0]
        summed_value = summed_value + returned[1]
    return (
        attn_out,
        grad_query,
        summed_key.astype(jnp.bfloat16),
        summed_value.astype(jnp.bfloat16),
    )


def solution(mesh):
    placed = (
        P(("seq", "pair"), None),
        P(("seq", "pair"), None),
        P(("seq", "pair"), None),
        P(("seq", "pair"), None),
        P(("seq", "pair")),
        P(),
        P(),
        P(),
    )
    return jax.shard_map(
        per_device,
        mesh=mesh,
        in_specs=placed,
        out_specs=(
            P(("seq", "pair"), None),
            P(("seq", "pair"), None),
            P(("seq", "pair"), None),
            P(("seq", "pair"), None),
        ),
        check_vma=False,
    )
```

profile of v0, /device:TPU:88, one launch (start us, length us, event | category | flops | bytes accessed | tf_op | source)
XLA Modules:
  0.0 565.9 jit_solution(4310030946616344261)
XLA Ops:
  1.4 3.0 collective-permute-start.13
  4.5 3.3 collective-permute-start.12
  7.7 3.6 collective-permute-start.11
  11.4 4.5 collective-permute-start.10
  15.9 2.4 collective-permute-start
  27.4 4.0 collective-permute-start.1
  32.7 2.9 collective-permute-start.9
  35.6 3.5 collective-permute-start.8
  39.1 3.9 collective-permute-start.2
  44.2 2.3 collective-permute-start.7
  46.5 4.7 collective-permute-start.3
  52.0 3.1 collective-permute-start.4
  58.2 7.0 %collective-permute-start.5 = (bf16[256,1024]{1,0:T(8,128)(2,1)S(1)}, bf16[256,1024]{1,0:T(8,128)(2,1)S(1)}, u32[]{:S(2)}, u32[]{:S(2)}) collective-permute-start(bf16[256,1024]{1,0:T(8,128)(2,1)S(1)} %copy-done.22), channel_id=1, source_target_pairs={{0,6},{1,7},{2,8},{3,9},{4,10},{5,11},{6,12},{7,13},{8,14},{9,15},... | collective-permute-start | bytes 1572872 | tf_op jit(solution)/shard_map/ppermute | solution.py:13
  66.1 7.4 %collective-permute-start.6 = (bf16[256,1024]{1,0:T(8,128)(2,1)S(1)}, bf16[256,1024]{1,0:T(8,128)(2,1)S(1)}, u32[]{:S(2)}, u32[]{:S(2)}) collective-permute-start(bf16[256,1024]{1,0:T(8,128)(2,1)S(1)} %copy-done.22), channel_id=1, source_target_pairs={{0,7},{1,8},{2,9},{3,10},{4,11},{5,12},{6,13},{7,14},{8,15},{9,16}... | collective-permute-start | bytes 1572872 | tf_op jit(solution)/shard_map/ppermute | solution.py:13
  80.0 4.2 collective-permute-start.16
  86.1 3.6 collective-permute-done.5
  89.7 12.6 %collective-permute-start.19 = (bf16[256,1024]{1,0:T(8,128)(2,1)S(1)}, bf16[256,1024]{1,0:T(8,128)(2,1)S(1)}, u32[]{:S(2)}, u32[]{:S(2)}) collective-permute-start(bf16[256,1024]{1,0:T(8,128)(2,1)S(1)} %copy-done.23), channel_id=1, source_target_pairs={{0,6},{1,7},{2,8},{3,9},{4,10},{5,11},{6,12},{7,13},{8,14},{9,15},... | collective-permute-start | bytes 1572872 | tf_op jit(solution)/shard_map/ppermute | solution.py:13
  103.2 3.8 collective-permute-start.18
  108.0 2.6 collective-permute-start.17
  110.7 10.0 %collective-permute-done.15 = bf16[256,1024]{1,0:T(8,128)(2,1)S(1)} collective-permute-done((bf16[256,1024]{1,0:T(8,128)(2,1)S(1)}, bf16[256,1024]{1,0:T(8,128)(2,1)S(1)}, u32[]{:S(2)}, u32[]{:S(2)}) %collective-permute-start.15) | collective-permute-done | bytes 524320 | tf_op jit(solution)/shard_map/ppermute | solution.py:13
  122.6 16.8 %collective-permute-done.16 = bf16[256,1024]{1,0:T(8,128)(2,1)S(1)} collective-permute-done((bf16[256,1024]{1,0:T(8,128)(2,1)S(1)}, bf16[256,1024]{1,0:T(8,128)(2,1)S(1)}, u32[]{:S(2)}, u32[]{:S(2)}) %collective-permute-start.16) | collective-permute-done | bytes 524320 | tf_op jit(solution)/shard_map/ppermute | solution.py:13
  139.5 2.4 fusion.3
  141.8 31.3 %collective-permute-done.17 = bf16[256,1024]{1,0:T(8,128)(2,1)S(1)} collective-permute-done((bf16[256,1024]{1,0:T(8,128)(2,1)S(1)}, bf16[256,1024]{1,0:T(8,128)(2,1)S(1)}, u32[]{:S(2)}, u32[]{:S(2)}) %collective-permute-start.17) | collective-permute-done | bytes 524320 | tf_op jit(solution)/shard_map/ppermute | solution.py:13
  180.5 34.5 %collective-permute-done.20 = bf16[256,1024]{1,0:T(8,128)(2,1)S(1)} collective-permute-done((bf16[256,1024]{1,0:T(8,128)(2,1)S(1)}, bf16[256,1024]{1,0:T(8,128)(2,1)S(1)}, u32[]{:S(2)}, u32[]{:S(2)}) %collective-permute-start.20) | collective-permute-done | bytes 524320 | tf_op jit(solution)/shard_map/ppermute | solution.py:13
  215.1 2.4 fusion.31
  217.6 2.3 fusion.30
  231.2 9.5 %fusion.47 = (bf16[256,2048]{0,1:T(8,128)(2,1)S(1)}, bf16[256,2048]{0,1:T(8,128)(2,1)S(1)}, bf16[256,2048]{0,1:T(8,128)(2,1)S(1)}, bf16[256,2048]{0,1:T(8,128)(2...) fusion(f32[]{:T(128)S(6)} %div.32, ...), kind=kOutput, calls=%fused_computation.95 | convolution fusion | flops 164626432 | bytes 25778696 | tf_op jit(solution)/shard_map/dot_general | solution.py:82
  253.3 2.4 fusion.155
  259.2 2.7 collective-permute-start.27
  261.9 4.6 collective-permute-start.26
  275.5 2.4 fusion.154
  280.0 35.7 %collective-permute-start.23 = (f32[256,1024]{0,1:T(8,128)S(1)}, f32[256,1024]{0,1:T(8,128)S(1)}, u32[]{:S(2)}, u32[]{:S(2)}) collective-permute-start(f32[256,1024]{0,1:T(8,128)S(1)} %get-tuple-element.24), channel_id=1, source_target_pairs={{3,0},{4,1},{5,2},{6,3},{7,4},{8,5},{9,6},{10,7},{11,8},{12,9},{13... | collective-permute-start | bytes 3145736 | tf_op jit(solution)/shard_map/ppermute | solution.py:13
  317.7 8.1 %collective-permute-start.28 = (f32[256,1024]{0,1:T(8,128)S(1)}, f32[256,1024]{0,1:T(8,128)S(1)}, u32[]{:S(2)}, u32[]{:S(2)}) collective-permute-start(f32[256,1024]{0,1:T(8,128)S(1)} %get-tuple-element.12), channel_id=1, source_target_pairs={{1,0},{2,1},{3,2},{4,3},{5,4},{6,5},{7,6},{8,7},{9,8},{10,9},{11,1... | collective-permute-start | bytes 3145736 | tf_op jit(solution)/shard_map/ppermute | solution.py:13
  325.8 22.6 %collective-permute-done.25 = f32[256,1024]{0,1:T(8,128)S(1)} collective-permute-done((f32[256,1024]{0,1:T(8,128)S(1)}, f32[256,1024]{0,1:T(8,128)S(1)}, u32[]{:S(2)}, u32[]{:S(2)}) %collective-permute-start.25) | collective-permute-done | bytes 1048608 | tf_op jit(solution)/shard_map/ppermute | solution.py:13
  350.3 2.3 fusion.70
  352.6 2.4 fusion.69
  359.3 14.6 %collective-permute-done.24 = f32[256,1024]{0,1:T(8,128)S(1)} collective-permute-done((f32[256,1024]{0,1:T(8,128)S(1)}, f32[256,1024]{0,1:T(8,128)S(1)}, u32[]{:S(2)}, u32[]{:S(2)}) %collective-permute-start.24) | collective-permute-done | bytes 1048608 | tf_op jit(solution)/shard_map/ppermute | solution.py:13
  373.9 10.4 %collective-permute-start.33 = (f32[256,1024]{0,1:T(8,128)}, f32[256,1024]{0,1:T(8,128)}, u32[]{:S(2)}, u32[]{:S(2)}) collective-permute-start(f32[256,1024]{0,1:T(8,128)} %get-tuple-element.14), channel_id=1, source_target_pairs={{6,0},{7,1},{8,2},{9,3},{10,4},{11,5},{12,6},{13,7},{14,8},{15,9},... | collective-permute-start | bytes 3145736 | tf_op jit(solution)/shard_map/ppermute | solution.py:13
  384.2 13.8 %collective-permute-done.23 = f32[256,1024]{0,1:T(8,128)S(1)} collective-permute-done((f32[256,1024]{0,1:T(8,128)S(1)}, f32[256,1024]{0,1:T(8,128)S(1)}, u32[]{:S(2)}, u32[]{:S(2)}) %collective-permute-start.23) | collective-permute-done | bytes 1048608 | tf_op jit(solution)/shard_map/ppermute | solution.py:13
  399.9 9.5 %collective-permute-done.22 = f32[256,1024]{0,1:T(8,128)S(1)} collective-permute-done((f32[256,1024]{0,1:T(8,128)S(1)}, f32[256,1024]{0,1:T(8,128)S(1)}, u32[]{:S(2)}, u32[]{:S(2)}) %collective-permute-start.22) | collective-permute-done | bytes 1048608 | tf_op jit(solution)/shard_map/ppermute | solution.py:13
  409.4 16.4 %collective-permute-start.31 = (f32[256,1024]{0,1:T(8,128)}, f32[256,1024]{0,1:T(8,128)}, u32[]{:S(2)}, u32[]{:S(2)}) collective-permute-start(f32[256,1024]{0,1:T(8,128)} %get-tuple-element.16), channel_id=1, source_target_pairs={{4,0},{5,1},{6,2},{7,3},{8,4},{9,5},{10,6},{11,7},{12,8},{13,9},{1... | collective-permute-start | bytes 3145736 | tf_op jit(solution)/shard_map/ppermute | solution.py:13
  425.9 16.4 %collective-permute-start.30 = (f32[256,1024]{0,1:T(8,128)S(1)}, f32[256,1024]{0,1:T(8,128)}, u32[]{:S(2)}, u32[]{:S(2)}) collective-permute-start(f32[256,1024]{0,1:T(8,128)S(1)} %get-tuple-element.17), channel_id=1, source_target_pairs={{3,0},{4,1},{5,2},{6,3},{7,4},{8,5},{9,6},{10,7},{11,8},{12,9},{13... | collective-permute-start | bytes 3145736 | tf_op jit(solution)/shard_map/ppermute | solution.py:13
  448.4 2.3 fusion.65
  454.8 3.8 fusion.85
  459.6 16.1 %collective-permute-done.31 = f32[256,1024]{0,1:T(8,128)} collective-permute-done((f32[256,1024]{0,1:T(8,128)}, f32[256,1024]{0,1:T(8,128)}, u32[]{:S(2)}, u32[]{:S(2)}) %collective-permute-start.31) | collective-permute-done | bytes 1048608 | tf_op jit(solution)/shard_map/ppermute | solution.py:13
  475.8 57.1 %collective-permute-done.30 = f32[256,1024]{0,1:T(8,128)} collective-permute-done((f32[256,1024]{0,1:T(8,128)S(1)}, f32[256,1024]{0,1:T(8,128)}, u32[]{:S(2)}, u32[]{:S(2)}) %collective-permute-start.30) | collective-permute-done | bytes 1048608 | tf_op jit(solution)/shard_map/ppermute | solution.py:13
  532.9 28.2 %collective-permute-done.29 = f32[256,1024]{0,1:T(8,128)} collective-permute-done((f32[256,1024]{0,1:T(8,128)S(1)}, f32[256,1024]{0,1:T(8,128)}, u32[]{:S(2)}, u32[]{:S(2)}) %collective-permute-start.29) | collective-permute-done | bytes 1048608 | tf_op jit(solution)/shard_map/ppermute | solution.py:13
  561.1 3.8 fusion.78
  (192 shorter events, 95.4 us)
Async XLA Ops:
  0.6 42.3 %copy-start.31 = (s32[128]{0:T(128)S(1)}, s32[128]{0:T(128)}, u32[]{:S(2)}) copy-start(s32[128]{0:T(128)} %param.14) | copy-start | bytes 1540
  1.4 25.9 %collective-permute-start.13 = (bf16[256]{0:T(256)(128)(2,1)S(1)}, bf16[256]{0:T(256)(128)(2,1)S(1)}, u32[]{:S(2)}, u32[]{:S(2)}) collective-permute-start(bf16[256]{0:T(256)(128)(2,1)S(1)} %get-tuple-element.35), channel_id=1, source_target_pairs={{0,7},{1,8},{2,9},{3,10},{4,11},{5,12},{6,13},{7,14},{8,15},{9,16}... | collective-permute-start | bytes 1544 | tf_op jit(solution)/shard_map/ppermute | solution.py:13
  4.5 28.2 %collective-permute-start.12 = (bf16[256]{0:T(256)(128)(2,1)S(1)}, bf16[256]{0:T(256)(128)(2,1)S(1)}, u32[]{:S(2)}, u32[]{:S(2)}) collective-permute-start(bf16[256]{0:T(256)(128)(2,1)S(1)} %get-tuple-element.35), channel_id=1, source_target_pairs={{0,6},{1,7},{2,8},{3,9},{4,10},{5,11},{6,12},{7,13},{8,14},{9,15},... | collective-permute-start | bytes 1544 | tf_op jit(solution)/shard_map/ppermute | solution.py:13
  7.7 27.8 %collective-permute-start.11 = (bf16[256]{0:T(256)(128)(2,1)S(1)}, bf16[256]{0:T(256)(128)(2,1)S(1)}, u32[]{:S(2)}, u32[]{:S(2)}) collective-permute-start(bf16[256]{0:T(256)(128)(2,1)S(1)} %get-tuple-element.35), channel_id=1, source_target_pairs={{0,5},{1,6},{2,7},{3,8},{4,9},{5,10},{6,11},{7,12},{8,13},{9,14},{... | collective-permute-start | bytes 1544 | tf_op jit(solution)/shard_map/ppermute | solution.py:13
  11.4 27.7 %collective-permute-start.10 = (bf16[256]{0:T(256)(128)(2,1)S(1)}, bf16[256]{0:T(256)(128)(2,1)S(1)}, u32[]{:S(2)}, u32[]{:S(2)}) collective-permute-start(bf16[256]{0:T(256)(128)(2,1)S(1)} %get-tuple-element.35), channel_id=1, source_target_pairs={{0,4},{1,5},{2,6},{3,7},{4,8},{5,9},{6,10},{7,11},{8,12},{9,13},{1... | collective-permute-start | bytes 1544 | tf_op jit(solution)/shard_map/ppermute | solution.py:13
  15.9 42.4 %collective-permute-start = (bf16[256,1024]{1,0:T(8,128)(2,1)}, bf16[256,1024]{1,0:T(8,128)(2,1)S(1)}, u32[]{:S(2)}, u32[]{:S(2)}) collective-permute-start(bf16[256,1024]{1,0:T(8,128)(2,1)} %param.9), channel_id=1, source_target_pairs={{0,1},{1,2},{2,3},{3,4},{4,5},{5,6},{6,7},{7,8},{8,9},{9,10},{10,1... | collective-permute-start | bytes 1572872 | tf_op jit(solution)/shard_map/ppermute | solution.py:13
  18.2 56.1 %copy-start.23 = (bf16[256,1024]{1,0:T(8,128)(2,1)S(1)}, bf16[256,1024]{1,0:T(8,128)(2,1)}, u32[]{:S(2)}) copy-start(bf16[256,1024]{1,0:T(8,128)(2,1)} %param.10) | copy-start | bytes 1572868
  27.4 38.7 %collective-permute-start.1 = (bf16[256,1024]{1,0:T(8,128)(2,1)S(1)}, bf16[256,1024]{1,0:T(8,128)(2,1)S(1)}, u32[]{:S(2)}, u32[]{:S(2)}) collective-permute-start(bf16[256,1024]{1,0:T(8,128)(2,1)S(1)} %copy-done.22), channel_id=1, source_target_pairs={{0,2},{1,3},{2,4},{3,5},{4,6},{5,7},{6,8},{7,9},{8,10},{9,11},{10,... | collective-permute-start | bytes 1572872 | tf_op jit(solution)/shard_map/ppermute | solution.py:13
  32.7 11.6 %collective-permute-start.9 = (bf16[256]{0:T(256)(128)(2,1)S(1)}, bf16[256]{0:T(256)(128)(2,1)S(1)}, u32[]{:S(2)}, u32[]{:S(2)}) collective-permute-start(bf16[256]{0:T(256)(128)(2,1)S(1)} %get-tuple-element.35), channel_id=1, source_target_pairs={{0,3},{1,4},{2,5},{3,6},{4,7},{5,8},{6,9},{7,10},{8,11},{9,12},{10... | collective-permute-start | bytes 1544 | tf_op jit(solution)/shard_map/ppermute | solution.py:13
  35.6 11.0 %collective-permute-start.8 = (bf16[256]{0:T(256)(128)(2,1)S(1)}, bf16[256]{0:T(256)(128)(2,1)S(1)}, u32[]{:S(2)}, u32[]{:S(2)}) collective-permute-start(bf16[256]{0:T(256)(128)(2,1)S(1)} %get-tuple-element.35), channel_id=1, source_target_pairs={{0,2},{1,3},{2,4},{3,5},{4,6},{5,7},{6,8},{7,9},{8,10},{9,11},{10,... | collective-permute-start | bytes 1544 | tf_op jit(solution)/shard_map/ppermute | solution.py:13
  39.1 35.3 %collective-permute-start.2 = (bf16[256,1024]{1,0:T(8,128)(2,1)S(1)}, bf16[256,1024]{1,0:T(8,128)(2,1)S(1)}, u32[]{:S(2)}, u32[]{:S(2)}) collective-permute-start(bf16[256,1024]{1,0:T(8,128)(2,1)S(1)} %copy-done.22), channel_id=1, source_target_pairs={{0,3},{1,4},{2,5},{3,6},{4,7},{5,8},{6,9},{7,10},{8,11},{9,12},{10... | collective-permute-start | bytes 1572872 | tf_op jit(solution)/shard_map/ppermute | solution.py:13
  44.2 7.7 %collective-permute-start.7 = (bf16[256]{0:T(256)(128)(2,1)S(1)}, bf16[256]{0:T(256)(128)(2,1)S(1)}, u32[]{:S(2)}, u32[]{:S(2)}) collective-permute-start(bf16[256]{0:T(256)(128)(2,1)S(1)} %get-tuple-element.35), channel_id=1, source_target_pairs={{0,1},{1,2},{2,3},{3,4},{4,5},{5,6},{6,7},{7,8},{8,9},{9,10},{10,1... | collective-permute-start | bytes 1544 | tf_op jit(solution)/shard_map/ppermute | solution.py:13
  46.5 30.6 %collective-permute-start.3 = (bf16[256,1024]{1,0:T(8,128)(2,1)S(1)}, bf16[256,1024]{1,0:T(8,128)(2,1)S(1)}, u32[]{:S(2)}, u32[]{:S(2)}) collective-permute-start(bf16[256,1024]{1,0:T(8,128)(2,1)S(1)} %copy-done.22), channel_id=1, source_target_pairs={{0,4},{1,5},{2,6},{3,7},{4,8},{5,9},{6,10},{7,11},{8,12},{9,13},{1... | collective-permute-start | bytes 1572872 | tf_op jit(solution)/shard_map/ppermute | solution.py:13
  52.0 28.1 %collective-permute-start.4 = (bf16[256,1024]{1,0:T(8,128)(2,1)S(1)}, bf16[256,1024]{1,0:T(8,128)(2,1)}, u32[]{:S(2)}, u32[]{:S(2)}) collective-permute-start(bf16[256,1024]{1,0:T(8,128)(2,1)S(1)} %copy-done.22), channel_id=1, source_target_pairs={{0,5},{1,6},{2,7},{3,8},{4,9},{5,10},{6,11},{7,12},{8,13},{9,14},{... | collective-permute-start | bytes 1572872 | tf_op jit(solution)/shard_map/ppermute | solution.py:13
  58.2 31.5 %collective-permute-start.5 = (bf16[256,1024]{1,0:T(8,128)(2,1)S(1)}, bf16[256,1024]{1,0:T(8,128)(2,1)S(1)}, u32[]{:S(2)}, u32[]{:S(2)}) collective-permute-start(bf16[256,1024]{1,0:T(8,128)(2,1)S(1)} %copy-done.22), channel_id=1, source_target_pairs={{0,6},{1,7},{2,8},{3,9},{4,10},{5,11},{6,12},{7,13},{8,14},{9,15},... | collective-permute-start | bytes 1572872 | tf_op jit(solution)/shard_map/ppermute | solution.py:13
  66.1 37.2 %collective-permute-start.6 = (bf16[256,1024]{1,0:T(8,128)(2,1)S(1)}, bf16[256,1024]{1,0:T(8,128)(2,1)S(1)}, u32[]{:S(2)}, u32[]{:S(2)}) collective-permute-start(bf16[256,1024]{1,0:T(8,128)(2,1)S(1)} %copy-done.22), channel_id=1, source_target_pairs={{0,7},{1,8},{2,9},{3,10},{4,11},{5,12},{6,13},{7,14},{8,15},{9,16}... | collective-permute-start | bytes 1572872 | tf_op jit(solution)/shard_map/ppermute | solution.py:13
  74.4 33.6 %collective-permute-start.14 = (bf16[256,1024]{1,0:T(8,128)(2,1)S(1)}, bf16[256,1024]{1,0:T(8,128)(2,1)S(1)}, u32[]{:S(2)}, u32[]{:S(2)}) collective-permute-start(bf16[256,1024]{1,0:T(8,128)(2,1)S(1)} %copy-done.23), channel_id=1, source_target_pairs={{0,1},{1,2},{2,3},{3,4},{4,5},{5,6},{6,7},{7,8},{8,9},{9,10},{10,1... | collective-permute-start | bytes 1572872 | tf_op jit(solution)/shard_map/ppermute | solution.py:13
  77.1 43.5 %collective-permute-start.15 = (bf16[256,1024]{1,0:T(8,128)(2,1)S(1)}, bf16[256,1024]{1,0:T(8,128)(2,1)S(1)}, u32[]{:S(2)}, u32[]{:S(2)}) collective-permute-start(bf16[256,1024]{1,0:T(8,128)(2,1)S(1)} %copy-done.23), channel_id=1, source_target_pairs={{0,2},{1,3},{2,4},{3,5},{4,6},{5,7},{6,8},{7,9},{8,10},{9,11},{10,... | collective-permute-start | bytes 1572872 | tf_op jit(solution)/shard_map/ppermute | solution.py:13
  80.0 59.4 %collective-permute-start.16 = (bf16[256,1024]{1,0:T(8,128)(2,1)S(1)}, bf16[256,1024]{1,0:T(8,128)(2,1)S(1)}, u32[]{:S(2)}, u32[]{:S(2)}) collective-permute-start(bf16[256,1024]{1,0:T(8,128)(2,1)S(1)} %copy-done.23), channel_id=1, source_target_pairs={{0,3},{1,4},{2,5},{3,6},{4,7},{5,8},{6,9},{7,10},{8,11},{9,12},{10... | collective-permute-start | bytes 1572872 | tf_op jit(solution)/shard_map/ppermute | solution.py:13
  89.7 88.3 %collective-permute-start.19 = (bf16[256,1024]{1,0:T(8,128)(2,1)S(1)}, bf16[256,1024]{1,0:T(8,128)(2,1)S(1)}, u32[]{:S(2)}, u32[]{:S(2)}) collective-permute-start(bf16[256,1024]{1,0:T(8,128)(2,1)S(1)} %copy-done.23), channel_id=1, source_target_pairs={{0,6},{1,7},{2,8},{3,9},{4,10},{5,11},{6,12},{7,13},{8,14},{9,15},... | collective-permute-start | bytes 1572872 | tf_op jit(solution)/shard_map/ppermute | solution.py:13
  103.2 36.2 %copy-start.19 = (bf16[256,1024]{1,0:T(8,128)(2,1)S(1)}, bf16[256,1024]{1,0:T(8,128)(2,1)}, u32[]{:S(2)}) copy-start(bf16[256,1024]{1,0:T(8,128)(2,1)} %param.8) | copy-start | bytes 1572868
  103.2 72.4 %collective-permute-start.18 = (bf16[256,1024]{1,0:T(8,128)(2,1)S(1)}, bf16[256,1024]{1,0:T(8,128)(2,1)S(1)}, u32[]{:S(2)}, u32[]{:S(2)}) collective-permute-start(bf16[256,1024]{1,0:T(8,128)(2,1)S(1)} %copy-done.23), channel_id=1, source_target_pairs={{0,5},{1,6},{2,7},{3,8},{4,9},{5,10},{6,11},{7,12},{8,13},{9,14},{... | collective-permute-start | bytes 1572872 | tf_op jit(solution)/shard_map/ppermute | solution.py:13
  108.0 65.1 %collective-permute-start.17 = (bf16[256,1024]{1,0:T(8,128)(2,1)S(1)}, bf16[256,1024]{1,0:T(8,128)(2,1)S(1)}, u32[]{:S(2)}, u32[]{:S(2)}) collective-permute-start(bf16[256,1024]{1,0:T(8,128)(2,1)S(1)} %copy-done.23), channel_id=1, source_target_pairs={{0,4},{1,5},{2,6},{3,7},{4,8},{5,9},{6,10},{7,11},{8,12},{9,13},{1... | collective-permute-start | bytes 1572872 | tf_op jit(solution)/shard_map/ppermute | solution.py:13
  120.6 94.4 %collective-permute-start.20 = (bf16[256,1024]{1,0:T(8,128)(2,1)S(1)}, bf16[256,1024]{1,0:T(8,128)(2,1)S(1)}, u32[]{:S(2)}, u32[]{:S(2)}) collective-permute-start(bf16[256,1024]{1,0:T(8,128)(2,1)S(1)} %copy-done.23), channel_id=1, source_target_pairs={{0,7},{1,8},{2,9},{3,10},{4,11},{5,12},{6,13},{7,14},{8,15},{9,16}... | collective-permute-start | bytes 1572872 | tf_op jit(solution)/shard_map/ppermute | solution.py:13
  179.3 35.9 %copy-start.20 = (bf16[256,1024]{1,0:T(8,128)(2,1)S(1)}, bf16[256,1024]{1,0:T(8,128)(2,1)}, u32[]{:S(2)}) copy-start(bf16[256,1024]{1,0:T(8,128)(2,1)} %param.11) | copy-start | bytes 1572868
  180.5 37.1 %copy-start.32 = (f32[256,2048]{0,1:T(8,128)}, f32[256,2048]{0,1:T(8,128)S(1)}, u32[]{:S(2)}) copy-start(f32[256,2048]{0,1:T(8,128)S(1)} %fusion.15) | copy-start | bytes 6291460
  257.1 22.9 %collective-permute-start.21 = (f32[256,1024]{0,1:T(8,128)}, f32[256,1024]{0,1:T(8,128)S(1)}, u32[]{:S(2)}, u32[]{:S(2)}) collective-permute-start(f32[256,1024]{0,1:T(8,128)} %get-tuple-element.19), channel_id=1, source_target_pairs={{1,0},{2,1},{3,2},{4,3},{5,4},{6,5},{7,6},{8,7},{9,8},{10,9},{11,1... | collective-permute-start | bytes 3145736 | tf_op jit(solution)/shard_map/ppermute | solution.py:13
  259.2 56.6 %collective-permute-start.27 = (f32[256,1024]{0,1:T(8,128)}, f32[256,1024]{0,1:T(8,128)S(1)}, u32[]{:S(2)}, u32[]{:S(2)}) collective-permute-start(f32[256,1024]{0,1:T(8,128)} %get-tuple-element.20), channel_id=1, source_target_pairs={{7,0},{8,1},{9,2},{10,3},{11,4},{12,5},{13,6},{14,7},{15,8},{16,9}... | collective-permute-start | bytes 3145736 | tf_op jit(solution)/shard_map/ppermute | solution.py:13
  261.9 55.8 %collective-permute-start.26 = (f32[256,1024]{0,1:T(8,128)S(1)}, f32[256,1024]{0,1:T(8,128)S(1)}, u32[]{:S(2)}, u32[]{:S(2)}) collective-permute-start(f32[256,1024]{0,1:T(8,128)S(1)} %get-tuple-element.21), channel_id=1, source_target_pairs={{6,0},{7,1},{8,2},{9,3},{10,4},{11,5},{12,6},{13,7},{14,8},{15,9},... | collective-permute-start | bytes 3145736 | tf_op jit(solution)/shard_map/ppermute | solution.py:13
  266.5 81.9 %collective-permute-start.25 = (f32[256,1024]{0,1:T(8,128)S(1)}, f32[256,1024]{0,1:T(8,128)S(1)}, u32[]{:S(2)}, u32[]{:S(2)}) collective-permute-start(f32[256,1024]{0,1:T(8,128)S(1)} %get-tuple-element.22), channel_id=1, source_target_pairs={{5,0},{6,1},{7,2},{8,3},{9,4},{10,5},{11,6},{12,7},{13,8},{14,9},{... | collective-permute-start | bytes 3145736 | tf_op jit(solution)/shard_map/ppermute | solution.py:13
  268.4 105.5 %collective-permute-start.24 = (f32[256,1024]{0,1:T(8,128)S(1)}, f32[256,1024]{0,1:T(8,128)S(1)}, u32[]{:S(2)}, u32[]{:S(2)}) collective-permute-start(f32[256,1024]{0,1:T(8,128)S(1)} %get-tuple-element.23), channel_id=1, source_target_pairs={{4,0},{5,1},{6,2},{7,3},{8,4},{9,5},{10,6},{11,7},{12,8},{13,9},{1... | collective-permute-start | bytes 3145736 | tf_op jit(solution)/shard_map/ppermute | solution.py:13
  280.0 75.1 %copy-start.17 = (bf16[256,2048]{0,1:T(8,128)(2,1)S(1)}, bf16[256,2048]{0,1:T(8,128)(2,1)}, u32[]{:S(2)}) copy-start(bf16[256,2048]{0,1:T(8,128)(2,1)} %get-tuple-element.30) | copy-start | bytes 3145732
  280.0 77.2 %copy-start.2 = (f32[256,1024]{0,1:T(8,128)}, f32[256,1024]{0,1:T(8,128)S(1)}, u32[]{:S(2)}) copy-start(f32[256,1024]{0,1:T(8,128)S(1)} %collective-permute-done.21) | copy-start | bytes 3145732
  280.0 118.0 %collective-permute-start.23 = (f32[256,1024]{0,1:T(8,128)S(1)}, f32[256,1024]{0,1:T(8,128)S(1)}, u32[]{:S(2)}, u32[]{:S(2)}) collective-permute-start(f32[256,1024]{0,1:T(8,128)S(1)} %get-tuple-element.24), channel_id=1, source_target_pairs={{3,0},{4,1},{5,2},{6,3},{7,4},{8,5},{9,6},{10,7},{11,8},{12,9},{13... | collective-permute-start | bytes 3145736 | tf_op jit(solution)/shard_map/ppermute | solution.py:13
  315.7 41.5 %copy-start.3 = (f32[256,1024]{0,1:T(8,128)}, f32[256,1024]{0,1:T(8,128)S(1)}, u32[]{:S(2)}) copy-start(f32[256,1024]{0,1:T(8,128)S(1)} %collective-permute-done.27) | copy-start | bytes 3145732
  315.7 93.7 %collective-permute-start.22 = (f32[256,1024]{0,1:T(8,128)S(1)}, f32[256,1024]{0,1:T(8,128)S(1)}, u32[]{:S(2)}, u32[]{:S(2)}) collective-permute-start(f32[256,1024]{0,1:T(8,128)S(1)} %get-tuple-element.25), channel_id=1, source_target_pairs={{2,0},{3,1},{4,2},{5,3},{6,4},{7,5},{8,6},{9,7},{10,8},{11,9},{12,... | collective-permute-start | bytes 3145736 | tf_op jit(solution)/shard_map/ppermute | solution.py:13
  317.7 39.5 %copy-start.4 = (f32[256,1024]{0,1:T(8,128)}, f32[256,1024]{0,1:T(8,128)S(1)}, u32[]{:S(2)}) copy-start(f32[256,1024]{0,1:T(8,128)S(1)} %collective-permute-done.26) | copy-start | bytes 3145732
  317.7 108.2 %collective-permute-start.28 = (f32[256,1024]{0,1:T(8,128)S(1)}, f32[256,1024]{0,1:T(8,128)S(1)}, u32[]{:S(2)}, u32[]{:S(2)}) collective-permute-start(f32[256,1024]{0,1:T(8,128)S(1)} %get-tuple-element.12), channel_id=1, source_target_pairs={{1,0},{2,1},{3,2},{4,3},{5,4},{6,5},{7,6},{8,7},{9,8},{10,9},{11,1... | collective-permute-start | bytes 3145736 | tf_op jit(solution)/shard_map/ppermute | solution.py:13
  348.4 93.9 %collective-permute-start.34 = (f32[256,1024]{0,1:T(8,128)S(1)}, f32[256,1024]{0,1:T(8,128)S(1)}, u32[]{:S(2)}, u32[]{:S(2)}) collective-permute-start(f32[256,1024]{0,1:T(8,128)S(1)} %get-tuple-element.13), channel_id=1, source_target_pairs={{7,0},{8,1},{9,2},{10,3},{11,4},{12,5},{13,6},{14,7},{15,8},{16,9}... | collective-permute-start | bytes 3145736 | tf_op jit(solution)/shard_map/ppermute | solution.py:13
  355.1 89.2 %copy-start.13 = (bf16[256,2048]{0,1:T(8,128)(2,1)S(1)}, bf16[256,2048]{0,1:T(8,128)(2,1)}, u32[]{:S(2)}) copy-start(bf16[256,2048]{0,1:T(8,128)(2,1)} %copy-done.12) | copy-start | bytes 3145732
  373.9 70.4 %copy-start.6 = (f32[256,1024]{0,1:T(8,128)}, f32[256,1024]{0,1:T(8,128)S(1)}, u32[]{:S(2)}) copy-start(f32[256,1024]{0,1:T(8,128)S(1)} %collective-permute-done.24) | copy-start | bytes 3145732
  373.9 85.8 %collective-permute-start.33 = (f32[256,1024]{0,1:T(8,128)}, f32[256,1024]{0,1:T(8,128)}, u32[]{:S(2)}, u32[]{:S(2)}) collective-permute-start(f32[256,1024]{0,1:T(8,128)} %get-tuple-element.14), channel_id=1, source_target_pairs={{6,0},{7,1},{8,2},{9,3},{10,4},{11,5},{12,6},{13,7},{14,8},{15,9},... | collective-permute-start | bytes 3145736 | tf_op jit(solution)/shard_map/ppermute | solution.py:13
  398.0 46.3 %copy-start.9 = (f32[256,1024]{0,1:T(8,128)}, f32[256,1024]{0,1:T(8,128)S(1)}, u32[]{:S(2)}) copy-start(f32[256,1024]{0,1:T(8,128)S(1)} %collective-permute-done.23) | copy-start | bytes 3145732
  398.0 61.6 %collective-permute-start.32 = (f32[256,1024]{0,1:T(8,128)}, f32[256,1024]{0,1:T(8,128)}, u32[]{:S(2)}, u32[]{:S(2)}) collective-permute-start(f32[256,1024]{0,1:T(8,128)} %get-tuple-element.15), channel_id=1, source_target_pairs={{5,0},{6,1},{7,2},{8,3},{9,4},{10,5},{11,6},{12,7},{13,8},{14,9},{... | collective-permute-start | bytes 3145736 | tf_op jit(solution)/shard_map/ppermute | solution.py:13
  409.4 34.9 %copy-start.10 = (f32[256,1024]{0,1:T(8,128)}, f32[256,1024]{0,1:T(8,128)S(1)}, u32[]{:S(2)}) copy-start(f32[256,1024]{0,1:T(8,128)S(1)} %collective-permute-done.22) | copy-start | bytes 3145732
  409.4 66.4 %collective-permute-start.31 = (f32[256,1024]{0,1:T(8,128)}, f32[256,1024]{0,1:T(8,128)}, u32[]{:S(2)}, u32[]{:S(2)}) collective-permute-start(f32[256,1024]{0,1:T(8,128)} %get-tuple-element.16), channel_id=1, source_target_pairs={{4,0},{5,1},{6,2},{7,3},{8,4},{9,5},{10,6},{11,7},{12,8},{13,9},{1... | collective-permute-start | bytes 3145736 | tf_op jit(solution)/shard_map/ppermute | solution.py:13
  425.9 107.0 %collective-permute-start.30 = (f32[256,1024]{0,1:T(8,128)S(1)}, f32[256,1024]{0,1:T(8,128)}, u32[]{:S(2)}, u32[]{:S(2)}) collective-permute-start(f32[256,1024]{0,1:T(8,128)S(1)} %get-tuple-element.17), channel_id=1, source_target_pairs={{3,0},{4,1},{5,2},{6,3},{7,4},{8,5},{9,6},{10,7},{11,8},{12,9},{13... | collective-permute-start | bytes 3145736 | tf_op jit(solution)/shard_map/ppermute | solution.py:13
  442.3 118.7 %collective-permute-start.29 = (f32[256,1024]{0,1:T(8,128)S(1)}, f32[256,1024]{0,1:T(8,128)}, u32[]{:S(2)}, u32[]{:S(2)}) collective-permute-start(f32[256,1024]{0,1:T(8,128)S(1)} %get-tuple-element.18), channel_id=1, source_target_pairs={{2,0},{3,1},{4,2},{5,3},{6,4},{7,5},{8,6},{9,7},{10,8},{11,9},{12,... | collective-permute-start | bytes 3145736 | tf_op jit(solution)/shard_map/ppermute | solution.py:13
  (21 other events, 330.0 us)
where the time goes:
time: 568 us; the launch traced here: 566 us
  waiting for transfers between devices  258 us (45%)
  starting transfers between devices  193 us (34%)
  matrix products  65.9 us (12%)
  local copies, waits for them, and re-layouts  29.7 us (5%)
  other arithmetic  16.3 us (3%)
    ppermute x35, waiting for transfers between devices, shifted(): lax.ppermute(value, axis, [(source, source + steps) for source in range(i...  258 us
    ppermute x35, starting transfers between devices, shifted(): lax.ppermute(value, axis, [(source, source + steps) for source in range(i...  193 us
    unnamed x94, local copies, waits for them, and re-layouts  22.9 us
    dot_general x8, matrix products, per_device(): lax.dot_general(query_head, key_head, contract_last, preferred_element_ty...  19 us
    dot_general x8, matrix products, per_device(): lax.dot_general(grad_head, value_head, contract_last, preferred_element_t...  18.3 us
    dot_general x8, matrix products, per_device(): jnp.dot(attn, value_head, preferred_element_type=jnp.float32)  16.7 us
  transfers between devices with their start and end apart: 35, of which 12 were waited for; matrix products, arithmetic and copies ran while one was open for 11% of the time, Pallas kernels for 0%

commit v1 on v0

v1 whole, which is shorter than its diff:
```python
import functools

import jax
import jax.numpy as jnp
from jax import lax
from jax.experimental import pallas as pl
from jax.experimental.pallas import tpu as pltpu
from jax.sharding import PartitionSpec as P

BLK = 256
HD = 128
RING = 8
MESH = pl.DeviceIdType.MESH
f32, bf16, i32 = jnp.float32, jnp.bfloat16, jnp.int32
SCALE = HD ** -0.5
NN = (((1,), (0,)), ((), ()))
NT = (((1,), (1,)), ((), ()))


def dot(a, b, dims=NN):
    return lax.dot_general(a, b, dims, preferred_element_type=f32)


def kernel(
    seqs, slope_ref, user_ref, length_ref, bucket_ref, q_hbm, k_hbm, v_hbm, g_hbm,
    o_out, dq_out, dk_out, dv_out,
    QB, KB, VB, GB, G_own, B_own, B_ring, B_cross, colB, rowB, inv,
    OJ, QJ, VI, KI, FJU, FJW, FIU, FIW,
    stage, cross_out, cross_in,
    load_sem, self_sem, in_send, in_recv, b_send, b_recv, x_send, x_recv, r_send, r_recv, o_send, o_recv, o_self,
):
    seq, pair = lax.axis_index("seq"), lax.axis_index("pair")
    blocks = seqs * RING
    y, core = pair // 2, pair % 2
    up, down = (seq + 1) % seqs, (seq + seqs - 1) % seqs
    outs = (o_out, dq_out, dk_out, dv_out)
    rings = (QB, KB, VB, GB)

    def place(k):
        return ((y + k // 2) % 4) * 2 + (core + k % 2) % 2

    def source(k):
        return ((y + 4 - k // 2) % 4) * 2 + (core + k % 2) % 2

    barrier = pltpu.get_barrier_semaphore()

    def greet(k, _):
        pl.semaphore_signal(barrier, inc=1, device_id=(seq, place(k)), device_id_type=MESH)
        return 0

    lax.fori_loop(1, RING, greet, 0)
    pl.semaphore_signal(barrier, inc=1, device_id=(up, pair), device_id_type=MESH)
    pl.semaphore_signal(barrier, inc=1, device_id=(down, pair), device_id_type=MESH)

    load = pltpu.make_async_copy(g_hbm, G_own, load_sem)
    load.start()

    def block_user(block):
        return user_ref[jnp.clip(block, 0, blocks - 1)]

    def live_rows(block):
        user = block_user(block)
        last = (block == blocks - 1) | (block_user(block + 1) != user)
        return jnp.where(last, lax.rem(length_ref[user] - 1, BLK) + 1, BLK)

    def prepare(p, _):
        zero = jnp.zeros((BLK, HD), f32)
        OJ[p] = zero
        QJ[p] = zero
        FJU[p] = zero
        FJW[p] = zero
        zero = jnp.zeros((HD, BLK), f32)
        VI[p] = zero
        KI[p] = zero
        FIU[p] = zero
        FIW[p] = zero

        @pl.when(p < 3)
        def _():
            FIU[8 + p] = zero
            FIW[8 + p] = zero

        length = length_ref[block_user(RING * seq + p)]
        inv[p] = 1.0 / jnp.full((8, BLK), length.astype(f32), f32)
        return 0

    lax.fori_loop(0, RING, prepare, 0)
    B_own[...] = jnp.broadcast_to(bucket_ref[...].astype(f32).reshape(1, BLK), (8, BLK))
    load.wait()
    own_live = live_rows(RING * seq + pair)

    def mask_own(n, _):
        rows = pl.ds(pl.multiple_of(n * 32, 32), 32)
        row = lax.broadcasted_iota(i32, (32, RING * HD), 0) + n * 32
        G_own[rows, :] = jnp.where(row < own_live, G_own[rows, :].astype(f32), 0.0).astype(bf16)
        return 0

    lax.fori_loop(0, BLK // 32, mask_own, 0)
    pl.semaphore_wait(barrier, RING + 1)

    sources = (q_hbm, k_hbm, v_hbm, G_own)

    def head(p):
        return pl.ds(pl.multiple_of(p * HD, HD), HD)

    def bucket_copy(k):
        return pltpu.make_async_remote_copy(
            B_own, B_ring.at[pair], b_send.at[k], b_recv.at[pair], device_id=(seq, place(k)), device_id_type=MESH)

    def in_copy(t, k):
        p = place(k)
        return pltpu.make_async_remote_copy(
            sources[t].at[:, head(p)], rings[t].at[pair], in_send.at[t, k], in_recv.at[t, pair],
            device_id=(seq, p), device_id_type=MESH)

    def self_copy(t):
        return pltpu.make_async_copy(sources[t].at[:, head(pair)], rings[t].at[pair], self_sem.at[t])

    for t in range(4):
        self_copy(t).start()
    self_bucket = pltpu.make_async_copy(B_own, B_ring.at[pair], self_sem.at[4])
    self_bucket.start()

    def send_two(first, second):
        def body(k, _):
            in_copy(first, k).start()
            in_copy(second, k).start()
            return 0

        lax.fori_loop(1, RING, body, 0)

    def send_buckets(k, _):
        bucket_copy(k).start()
        return 0

    lax.fori_loop(1, RING, send_buckets, 0)

    @pl.when(pair >= 4)
    def _():
        send_two(1, 2)
        send_two(0, 3)

    @pl.when(pair < 4)
    def _():
        send_two(0, 3)
        send_two(1, 2)

    for t in range(4):
        self_copy(t).wait()
    self_bucket.wait()

    def wait_in(t, p):
        pltpu.make_async_copy(rings[t].at[p], rings[t].at[p], in_recv.at[t, p]).wait()

    def cross_copies(p, upward):
        if upward:
            pairs = ((KB.at[p], KB.at[p + 4]), (VB.at[p], VB.at[p + 4]), (B_ring.at[p], B_cross.at[p]))
            to = (up, pair)
        else:
            pairs = ((QB.at[p], QB.at[p + 8]), (GB.at[p], GB.at[p + 8]), (B_ring.at[p], B_cross.at[p]))
            to = (down, pair)
        return [
            pltpu.make_async_remote_copy(
                src, dst, x_send.at[n, p], x_recv.at[n, p], device_id=to, device_id_type=MESH)
            for n, (src, dst) in enumerate(pairs)
        ]

    def pass_on(k, _):
        p = source(k)

        @pl.when(k > 0)
        def _():
            pltpu.make_async_copy(B_ring.at[p], B_ring.at[p], b_recv.at[p]).wait()

        @pl.when(p >= 4)
        def _():
            @pl.when(k > 0)
            def _():
                wait_in(1, p)
                wait_in(2, p)

            for copy in cross_copies(p, True):
                copy.start()

        @pl.when(p < 4)
        def _():
            @pl.when(k > 0)
            def _():
                wait_in(0, p)
                wait_in(3, p)

            @pl.when(p < 3)
            def _():
                for copy in cross_copies(p, False):
                    copy.start()

        return 0

    lax.fori_loop(0, RING, pass_on, 0)

    half_slope = 0.5 * slope_ref[pair]

    def arrive(k):
        p = source(k)

        @pl.when(k > 0)
        def _():
            @pl.when(p >= 4)
            def _():
                wait_in(0, p)
                wait_in(3, p)

            @pl.when(p < 4)
            def _():
                wait_in(1, p)
                wait_in(2, p)

        row = B_ring[p] * half_slope
        rowB[p] = row
        colB[p] = jnp.broadcast_to(row[0:1], (HD, BLK)).T

        @pl.when(p >= 4)
        def _():
            for copy in cross_copies(p, True):
                copy.wait_recv()
            crossed = B_cross[p] * half_slope
            colB[p + 4] = jnp.broadcast_to(crossed[0:1], (HD, BLK)).T

        @pl.when(p < 3)
        def _():
            for copy in cross_copies(p, False):
                copy.wait_recv()
            rowB[p + 8] = B_cross[p] * half_slope

    def tile(xj, yj, xi, yi, column, row, weight, mask=None):
        gap = jnp.abs(jnp.concatenate([column, column], axis=1) - row)
        half = dot(xj, xi, NT) * (0.5 * SCALE) - gap
        th = jnp.tanh(half)
        pw = th * weight + weight
        if mask is not None:
            pw = jnp.where(mask, pw, 0.0)
        aw = half * pw
        attn = aw.astype(bf16)
        bend = pw + aw * (1.0 - th)
        score = (dot(yj, yi, NT) * bend).astype(bf16)
        return (dot(attn, yi), dot(score, xi), dot(yj.T, attn), dot(xj.T, score))

    def diagonal(p):
        mask = lax.broadcasted_iota(i32, (BLK, BLK), 0) >= lax.broadcasted_iota(i32, (BLK, BLK), 1)
        uj, wj, ui, wi = tile(QB[p], GB[p], KB[p], VB[p], colB[p], rowB[p][0:1], inv[p][0:1], mask)
        OJ[p] += uj
        QJ[p] += wj
        VI[p] += ui
        KI[p] += wi

    def slot(p, r):
        j, i = jnp.maximum(p, r), jnp.minimum(p, r)
        upper = j >= 4
        ja = jnp.where(upper, j + 4, j)
        ia = jnp.where(upper, i, i + 8)
        base = RING * seq
        user_i, user_j = block_user(base + i), block_user(base + j)
        inside = user_i == user_j
        below = (block_user(base + j - 8) == user_i) & (seq > 0)
        above = (block_user(base + i + 8) == user_j) & (seq < seqs - 1)
        flag = jnp.where(upper, below, above)
        valid = jnp.where(inside | flag, 1.0, 0.0)
        on = jnp.where(flag, 1.0, 0.0)
        off = 1.0 - on
        weight = inv[jnp.where(upper, i, j)][0:1] * valid

        def pick(a, b):
            return lax.select(flag, a, b)

        uj, wj, ui, wi = tile(
            pick(KB[ja], QB[j]), pick(VB[ja], GB[j]), pick(QB[ia], KB[i]), pick(GB[ia], VB[i]),
            pick(colB[ja], colB[j]), pick(rowB[ia], rowB[i])[0:1], weight)
        OJ[j] += uj * off
        QJ[j] += wj * off
        FJU[j] += uj * on
        FJW[j] += wj * on
        VI[i] += ui * off
        KI[i] += wi * off
        FIU[ia] += ui * on
        FIW[ia] += wi * on

    back = 0.5 * SCALE

    def out_copy(t, p):
        return pltpu.make_async_remote_copy(
            stage.at[t, p], outs[t].at[:, head(pair)], o_send.at[t, p], o_recv.at[t, pair],
            device_id=(seq, p), device_id_type=MESH)

    def out_self(t):
        return pltpu.make_async_copy(stage.at[t, pair], outs[t].at[:, head(pair)], o_self.at[t])

    def emit(t, p):
        @pl.when(p != pair)
        def _():
            out_copy(t, p).start()

        @pl.when(p == pair)
        def _():
            out_self(t).start()

    def return_copies(p, downward):
        to = (down, pair) if downward else (up, pair)
        return [
            pltpu.make_async_remote_copy(
                cross_out.at[n, p], cross_in.at[n, p], r_send.at[n, p], r_recv.at[n, p],
                device_id=to, device_id_type=MESH)
            for n in range(2)
        ]

    def live_mask(p):
        return lax.broadcasted_iota(i32, (BLK, HD), 0) < live_rows(RING * seq + p)

    def finish(p):
        o = OJ[p] + FIU[p].T
        dq = (QJ[p] + FIW[p].T) * back
        dv = VI[p].T
        dk = KI[p].T * back

        @pl.when(p >= 4)
        def _():
            cross_out[0, p] = FJU[p].astype(bf16)
            cross_out[1, p] = (FJW[p] * back).astype(bf16)
            for copy in return_copies(p, True):
                copy.start()
            FJU[p] = dv
            FJW[p] = dk

        @pl.when(p < 3)
        def _():
            cross_out[0, p] = FIU[p + 8].T.astype(bf16)
            cross_out[1, p] = (FIW[p + 8].T * back).astype(bf16)
            for copy in return_copies(p, False):
                copy.start()
            OJ[p] = o
            QJ[p] = dq

        @pl.when(p >= 3)
        def _():
            stage[0, p] = jnp.where(live_mask(p), o, 0.0).astype(bf16)
            stage[1, p] = dq.astype(bf16)
            emit(0, p)
            emit(1, p)

        @pl.when(p < 4)
        def _():
            stage[2, p] = (dk + FJW[p] * back).astype(bf16)
            stage[3, p] = (dv + FJU[p]).astype(bf16)
            emit(2, p)
            emit(3, p)

    def step(k, _):
        arrive(k)
        p = source(k)

        def two(m, _):
            slot(p, source(2 * m))
            slot(p, source(2 * m + 1))
            return 0

        lax.fori_loop(0, k // 2, two, 0)

        @pl.when(k % 2 == 1)
        def _():
            slot(p, source(k - 1))
            diagonal(p)

        @pl.when(k % 2 == 0)
        def _():
            diagonal(p)

        return 0

    lax.fori_loop(0, RING - 1, step, 0)
    arrive(RING - 1)
    last = source(RING - 1)

    def last_two(m, _):
        slot(last, source(2 * m))
        slot(last, source(2 * m + 1))
        finish(source(2 * m))
        finish(source(2 * m + 1))
        return 0

    lax.fori_loop(0, 3, last_two, 0)
    slot(last, source(6))
    diagonal(last)
    finish(source(6))
    finish(last)

    def settle(k, _):
        p = source(k)

        @pl.when(p >= 4)
        def _():
            for copy in return_copies(p, True):
                copy.wait_recv()
            stage[2, p] = (FJW[p] + cross_in[1, p].astype(f32)).astype(bf16)
            stage[3, p] = (FJU[p] + cross_in[0, p].astype(f32)).astype(bf16)
            emit(2, p)
            emit(3, p)

        @pl.when(p < 3)
        def _():
            for copy in return_copies(p, False):
                copy.wait_recv()
            stage[0, p] = jnp.where(live_mask(p), OJ[p] + cross_in[0, p].astype(f32), 0.0).astype(bf16)
            stage[1, p] = (QJ[p] + cross_in[1, p].astype(f32)).astype(bf16)
            emit(0, p)
            emit(1, p)

        return 0

    lax.fori_loop(0, RING, settle, 0)

    def drain(k, _):
        p = source(k)

        @pl.when(p >= 4)
        def _():
            for copy in cross_copies(p, True) + return_copies(p, True):
                copy.wait_send()

        @pl.when(p < 3)
        def _():
            for copy in cross_copies(p, False) + return_copies(p, False):
                copy.wait_send()

        @pl.when(k > 0)
        def _():
            bucket_copy(k).wait_send()
            for t in range(4):
                in_copy(t, k).wait_send()
                out_copy(t, p).wait_send()
                pltpu.make_async_copy(stage.at[t, p], outs[t].at[:, head(p)], o_recv.at[t, p]).wait()

        return 0

    lax.fori_loop(0, RING, drain, 0)
    for t in range(4):
        out_self(t).wait()


def per_device(seqs, queries, keys, values, out_grad, event_bucket, slope, block_user, lengths):
    wide = jax.ShapeDtypeStruct((BLK, RING * HD), bf16)
    smem = pl.BlockSpec(memory_space=pltpu.SMEM)
    vmem = pl.BlockSpec(memory_space=pltpu.VMEM)
    hbm = pl.BlockSpec(memory_space=pl.ANY)
    down = lambda n: pltpu.VMEM((n, BLK, HD), f32)
    across = lambda n: pltpu.VMEM((n, HD, BLK), f32)
    dma = pltpu.SemaphoreType.DMA
    return pl.pallas_call(
        functools.partial(kernel, seqs),
        out_shape=(wide,) * 4,
        in_specs=[smem, smem, smem, vmem, hbm, hbm, hbm, hbm],
        out_specs=(hbm,) * 4,
        scratch_shapes=[
            pltpu.VMEM((11, BLK, HD), bf16),
            pltpu.VMEM((12, BLK, HD), bf16),
            pltpu.VMEM((12, BLK, HD), bf16),
            pltpu.VMEM((11, BLK, HD), bf16),
            pltpu.VMEM((BLK, RING * HD), bf16),
            pltpu.VMEM((8, BLK), f32),
            pltpu.VMEM((8, 8, BLK), f32),
            pltpu.VMEM((8, 8, BLK), f32),
            down(12),
            pltpu.VMEM((11, 8, BLK), f32),
            pltpu.VMEM((8, 8, BLK), f32),
            down(8), down(8), across(8), across(8), down(8), down(8), across(11), across(11),
            pltpu.VMEM((4, 8, BLK, HD), bf16),
            pltpu.VMEM((2, 8, BLK, HD), bf16),
            pltpu.VMEM((2, 8, BLK, HD), bf16),
            dma, dma((5,)), dma((4, 8)), dma((4, 8)), dma((8,)), dma((8,)), dma((3, 8)), dma((3, 8)),
            dma((2, 8)), dma((2, 8)), dma((4, 8)), dma((4, 8)), dma((4,)),
        ],
        compiler_params=pltpu.CompilerParams(
            collective_id=0, has_side_effects=True, vmem_limit_bytes=48 * 2**20),
        cost_estimate=pl.CostEstimate(
            flops=36 * 6 * 2 * BLK * BLK * HD, bytes_accessed=8 * BLK * RING * HD * 2, transcendentals=36 * BLK * BLK),
    )(slope, block_user, lengths, event_bucket, queries, keys, values, out_grad)


def solution(mesh):
    spread = P(("seq", "pair"), None)
    return jax.shard_map(
        functools.partial(per_device, mesh.shape["seq"]),
        mesh=mesh,
        in_specs=(spread, spread, spread, spread, P(("seq", "pair")), P(), P(), P()),
        out_specs=(spread,) * 4,
        check_vma=False,
    )
```

time: 568 us -> 81.3 us (0.14)
  the two profiles are of different devices: /device:TPU:88 before, /device:TPU:0 now
where the time goes in v1:
time: 81.3 us; the launch traced here: 80 us
  Pallas kernels  69.3 us (85%)
  local copies, waits for them, and re-layouts  9.97 us (12%)
    pallas_call x1, Pallas kernels, per_device(): pl.pallas_call(functools.partial(kernel, seqs), out_shape=(wide,) * 4, in...  69.3 us
    unnamed x20, local copies, waits for them, and re-layouts  9.97 us

profile of v1, /device:TPU:0, one launch (start us, length us, event | category | flops | bytes accessed | tf_op | source)
XLA Modules:
  0.0 80.0 jit_solution(7009914066696535960)
XLA Ops:
  0.6 0.0 copy-start
  0.6 1.0 %copy-done = bf16[256,1024]{1,0:T(8,128)(2,1)S(1)} copy-done((bf16[256,1024]{1,0:T(8,128)(2,1)S(1)}, bf16[256,1024]{1,0:T(8,128)(2,1)}, u32[]{:S(2)}) %copy-start) | copy-done | bytes 524312
  1.7 0.0 copy-start.1
  1.7 1.0 %copy-done.1 = bf16[256,1024]{1,0:T(8,128)(2,1)S(1)} copy-done((bf16[256,1024]{1,0:T(8,128)(2,1)S(1)}, bf16[256,1024]{1,0:T(8,128)(2,1)}, u32[]{:S(2)}) %copy-start.1) | copy-done | bytes 524312
  2.7 0.0 copy-start.2
  2.7 1.0 %copy-done.2 = bf16[256,1024]{1,0:T(8,128)(2,1)S(1)} copy-done((bf16[256,1024]{1,0:T(8,128)(2,1)S(1)}, bf16[256,1024]{1,0:T(8,128)(2,1)}, u32[]{:S(2)}) %copy-start.2) | copy-done | bytes 524312
  3.8 0.0 copy-start.3
  3.8 1.0 %copy-done.3 = bf16[256,1024]{1,0:T(8,128)(2,1)S(1)} copy-done((bf16[256,1024]{1,0:T(8,128)(2,1)S(1)}, bf16[256,1024]{1,0:T(8,128)(2,1)}, u32[]{:S(2)}) %copy-start.3) | copy-done | bytes 524312
  4.8 0.0 copy-start.4
  4.8 0.7 copy-done.4
  5.5 0.0 copy-start.5
  5.5 0.7 copy-done.5
  6.1 0.0 copy-start.6
  6.1 0.7 copy-done.6
  6.8 0.0 copy-start.7
  6.8 0.7 copy-done.7
  7.4 69.3 %shard_map.111 = (bf16[256,1024]{1,0:T(8,128)(2,1)S(1)}, bf16[256,1024]{1,0:T(8,128)(2,1)S(1)}, bf16[256,1024]{1,0:T(8,128)(2,1)S(1)}, bf16[256,1024]{1,0:T(8,128)(2,1)S(1)}) custom-call(f32[8]{0:T(128)S(1)} %copy-done.5, s32[128]{0:T(128)S(1)} %copy-done.6, s32[32]{0:T(128)S(1)} %copy-done.7, s32[256]{0:T(256)S(1)} %copy-done.4, ...), custom_call_target="tpu_custom_call" | custom-call | flops 3623878656 | bytes 4194304 | tf_op jit(solution)/shard_map/pallas_call | solution.py:456
  76.8 0.8 copy.16
  77.6 0.8 copy.17
  78.4 0.8 copy.18
  79.2 0.8 copy.19
Async XLA Ops:
  0.6 1.0 %copy-start = (bf16[256,1024]{1,0:T(8,128)(2,1)S(1)}, bf16[256,1024]{1,0:T(8,128)(2,1)}, u32[]{:S(2)}) copy-start(bf16[256,1024]{1,0:T(8,128)(2,1)} %q_hbm.1) | copy-start | bytes 1572868
  1.7 1.0 %copy-start.1 = (bf16[256,1024]{1,0:T(8,128)(2,1)S(1)}, bf16[256,1024]{1,0:T(8,128)(2,1)}, u32[]{:S(2)}) copy-start(bf16[256,1024]{1,0:T(8,128)(2,1)} %k_hbm.1) | copy-start | bytes 1572868
  2.7 1.0 %copy-start.2 = (bf16[256,1024]{1,0:T(8,128)(2,1)S(1)}, bf16[256,1024]{1,0:T(8,128)(2,1)}, u32[]{:S(2)}) copy-start(bf16[256,1024]{1,0:T(8,128)(2,1)} %v_hbm.1) | copy-start | bytes 1572868
  3.8 1.0 %copy-start.3 = (bf16[256,1024]{1,0:T(8,128)(2,1)S(1)}, bf16[256,1024]{1,0:T(8,128)(2,1)}, u32[]{:S(2)}) copy-start(bf16[256,1024]{1,0:T(8,128)(2,1)} %g_hbm.1) | copy-start | bytes 1572868
  4.8 0.7 copy-start.4
  5.5 0.7 copy-start.5
  6.1 0.7 copy-start.6
  6.8 0.7 copy-start.7

commit v2 on v1

--- a/solution.py
+++ b/solution.py
@@ -10,6 +10,7 @@
 BLK = 256
 HD = 128
 RING = 8
+WHOLE = 5
 MESH = pl.DeviceIdType.MESH
 f32, bf16, i32 = jnp.float32, jnp.bfloat16, jnp.int32
 SCALE = HD ** -0.5
@@ -22,12 +23,12 @@
 
 
 def kernel(
-    seqs, slope_ref, user_ref, length_ref, bucket_ref, q_hbm, k_hbm, v_hbm, g_hbm,
+    seqs, slope_hbm, user_hbm, length_hbm, bucket_hbm, q_hbm, k_hbm, v_hbm, g_hbm,
     o_out, dq_out, dk_out, dv_out,
-    QB, KB, VB, GB, G_own, B_own, B_ring, B_cross, colB, rowB, inv,
+    slope_ref, user_ref, length_ref, bucket_ref, QB, KB, VB, GB, G_own, B_own, B_ring, B_cross, colB, rowB, inv,
     OJ, QJ, VI, KI, FJU, FJW, FIU, FIW,
     stage, cross_out, cross_in,
-    load_sem, self_sem, in_send, in_recv, b_send, b_recv, x_send, x_recv, r_send, r_recv, o_send, o_recv, o_self,
+    load_sem, small_sem, self_sem, in_send, in_recv, b_send, b_recv, x_send, x_recv, r_send, r_recv, o_send, o_recv, o_self,
 ):
     seq, pair = lax.axis_index("seq"), lax.axis_index("pair")
     blocks = seqs * RING
@@ -36,11 +37,18 @@
     outs = (o_out, dq_out, dk_out, dv_out)
     rings = (QB, KB, VB, GB)
 
+    def offset(k):
+        dy = jnp.where(k < 2, 0, jnp.where(k < 6, 1 + 2 * (k % 2), 2))
+        dc = jnp.where(k < 2, k, jnp.where(k < 6, k // 4, k - 6))
+        return dy, dc
+
     def place(k):
-        return ((y + k // 2) % 4) * 2 + (core + k % 2) % 2
+        dy, dc = offset(k)
+        return ((y + dy) % 4) * 2 + (core + dc) % 2
 
     def source(k):
-        return ((y + 4 - k // 2) % 4) * 2 + (core + k % 2) % 2
+        dy, dc = offset(k)
+        return ((y + 4 - dy) % 4) * 2 + (core + dc) % 2
 
     barrier = pltpu.get_barrier_semaphore()
 
@@ -54,6 +62,15 @@
 
     load = pltpu.make_async_copy(g_hbm, G_own, load_sem)
     load.start()
+    smalls = [
+        pltpu.make_async_copy(src, dst, small_sem.at[n])
+        for n, (src, dst) in enumerate((
+            (user_hbm, user_ref), (length_hbm, length_ref), (slope_hbm, slope_ref), (bucket_hbm, bucket_ref)))
+    ]
+    for small in smalls:
+        small.start()
+    for small in smalls:
+        small.wait()
 
     def block_user(block):
         return user_ref[jnp.clip(block, 0, blocks - 1)]
@@ -121,13 +138,18 @@
     self_bucket = pltpu.make_async_copy(B_own, B_ring.at[pair], self_sem.at[4])
     self_bucket.start()
 
-    def send_two(first, second):
-        def body(k, _):
-            in_copy(first, k).start()
-            in_copy(second, k).start()
-            return 0
-
-        lax.fori_loop(1, RING, body, 0)
+    def send_order(first, second):
+        def send(*tensors):
+            def body(k, _):
+                for t in tensors:
+                    in_copy(t, k).start()
+                return 0
+
+            return body
+
+        lax.fori_loop(1, WHOLE + 1, send(*first, *second), 0)
+        lax.fori_loop(WHOLE + 1, RING, send(*first), 0)
+        lax.fori_loop(WHOLE + 1, RING, send(*second), 0)
 
     def send_buckets(k, _):
         bucket_copy(k).start()
@@ -137,13 +159,11 @@
 
     @pl.when(pair >= 4)
     def _():
-        send_two(1, 2)
-        send_two(0, 3)
+        send_order((1, 2), (0, 3))
 
     @pl.when(pair < 4)
     def _():
-        send_two(0, 3)
-        send_two(1, 2)
+        send_order((0, 3), (1, 2))
 
     for t in range(4):
         self_copy(t).wait()
@@ -196,7 +216,6 @@
 
         return 0
 
-    lax.fori_loop(0, RING, pass_on, 0)
 
     half_slope = 0.5 * slope_ref[pair]
 
@@ -375,25 +394,60 @@
 
         return 0
 
-    lax.fori_loop(0, RING - 1, step, 0)
+    def advance(k, _):
+        first = jnp.where(k == 0, 0, jnp.where(k < 4, 4, jnp.where(k < 6, k, 7)))
+        first = jnp.where(k == 5, 6, first)
+        end = jnp.where(k < 4, 4, jnp.where(k == 4, 6, jnp.where(k == 5, 7, 8)))
+        lax.fori_loop(first, end, pass_on, 0)
+        step(k, 0)
+        return 0
+
+    lax.fori_loop(0, RING - 1, advance, 0)
     arrive(RING - 1)
     last = source(RING - 1)
 
+    def turn(m):
+        return source(jnp.where(m < 5, m + 2, 6 - m))
+
     def last_two(m, _):
-        slot(last, source(2 * m))
-        slot(last, source(2 * m + 1))
-        finish(source(2 * m))
-        finish(source(2 * m + 1))
+        one, two = turn(2 * m), turn(2 * m + 1)
+        slot(last, one)
+        slot(last, two)
+        finish(one)
+        finish(two)
         return 0
 
     lax.fori_loop(0, 3, last_two, 0)
-    slot(last, source(6))
+    slot(last, turn(6))
     diagonal(last)
-    finish(source(6))
     finish(last)
+    finish(turn(6))
+
+    def drain_in(k, _):
+        p = source(k)
+
+        @pl.when(p >= 4)
+        def _():
+            for copy in cross_copies(p, True):
+                copy.wait_send()
+
+        @pl.when(p < 3)
+        def _():
+            for copy in cross_copies(p, False):
+                copy.wait_send()
+
+        @pl.when(k > 0)
+        def _():
+            bucket_copy(k).wait_send()
+            for t in range(4):
+                in_copy(t, k).wait_send()
+
+        return 0
+
+    lax.fori_loop(0, RING, drain_in, 0)
 
     def settle(k, _):
-        p = source(k)
+        p = source((k + 2) % RING)
 
         @pl.when(p >= 4)
         def _():
@@ -417,48 +471,69 @@
 
     lax.fori_loop(0, RING, settle, 0)
 
-    def drain(k, _):
+    def drain_out(k, _):
         p = source(k)
 
         @pl.when(p >= 4)
         def _():
-            for copy in cross_copies(p, True) + return_copies(p, True):
+            for copy in return_copies(p, True):
                 copy.wait_send()
 
         @pl.when(p < 3)
         def _():
-            for copy in cross_copies(p, False) + return_copies(p, False):
+            for copy in return_copies(p, False):
                 copy.wait_send()
 
         @pl.when(k > 0)
         def _():
-            bucket_copy(k).wait_send()
             for t in range(4):
-                in_copy(t, k).wait_send()
                 out_copy(t, p).wait_send()
                 pltpu.make_async_copy(stage.at[t, p], outs[t].at[:, head(p)], o_recv.at[t, p]).wait()
 
         return 0
 
-    lax.fori_loop(0, RING, drain, 0)
     for t in range(4):
         out_self(t).wait()
+    lax.fori_loop(0, RING, drain_out, 0)
+
+
+def hand_over(*refs):
+    ins, outs, held, load, store = refs[:4], refs[4:8], refs[8], refs[9], refs[10]
+    half = BLK // 2
+
+    def loads(n):
+        rows = pl.ds(n % 2 * half, half)
+        return pltpu.make_async_copy(ins[n // 2].at[rows, :], held.at[n], load.at[n])
+
+    def stores(n):
+        rows = pl.ds(n % 2 * half, half)
+        return pltpu.make_async_copy(held.at[n], outs[n // 2].at[rows, :], store.at[n])
+
+    for n in range(8):
+        loads(n).start()
+    for n in range(8):
+        loads(n).wait()
+        stores(n).start()
+    for n in range(8):
+        stores(n).wait()
 
 
 def per_device(seqs, queries, keys, values, out_grad, event_bucket, slope, block_user, lengths):
     wide = jax.ShapeDtypeStruct((BLK, RING * HD), bf16)
-    smem = pl.BlockSpec(memory_space=pltpu.SMEM)
-    vmem = pl.BlockSpec(memory_space=pltpu.VMEM)
     hbm = pl.BlockSpec(memory_space=pl.ANY)
     down = lambda n: pltpu.VMEM((n, BLK, HD), f32)
     across = lambda n: pltpu.VMEM((n, HD, BLK), f32)
     dma = pltpu.SemaphoreType.DMA
-    return pl.pallas_call(
+    results = pl.pallas_call(
         functools.partial(kernel, seqs),
         out_shape=(wide,) * 4,
-        in_specs=[smem, smem, smem, vmem, hbm, hbm, hbm, hbm],
+        in_specs=[hbm] * 8,
         out_specs=(hbm,) * 4,
         scratch_shapes=[
+            pltpu.SMEM((RING,), f32),
+            pltpu.SMEM((seqs * RING,), i32),
+            pltpu.SMEM(lengths.shape, i32),
+            pltpu.VMEM((BLK,), i32),
             pltpu.VMEM((11, BLK, HD), bf16),
             pltpu.VMEM((12, BLK, HD), bf16),
             pltpu.VMEM((12, BLK, HD), bf16),
@@ -474,14 +549,22 @@
             pltpu.VMEM((4, 8, BLK, HD), bf16),
             pltpu.VMEM((2, 8, BLK, HD), bf16),
             pltpu.VMEM((2, 8, BLK, HD), bf16),
-            dma, dma((5,)), dma((4, 8)), dma((4, 8)), dma((8,)), dma((8,)), dma((3, 8)), dma((3, 8)),
+            dma, dma((4,)), dma((5,)), dma((4, 8)), dma((4, 8)), dma((8,)), dma((8,)), dma((3, 8)), dma((3, 8)),
             dma((2, 8)), dma((2, 8)), dma((4, 8)), dma((4, 8)), dma((4,)),
         ],
         compiler_params=pltpu.CompilerParams(
-            collective_id=0, has_side_effects=True, vmem_limit_bytes=48 * 2**20),
+            collective_id=0, has_side_effects=True, vmem_limit_bytes=62 * 2**20),
         cost_estimate=pl.CostEstimate(
             flops=36 * 6 * 2 * BLK * BLK * HD, bytes_accessed=8 * BLK * RING * HD * 2, transcendentals=36 * BLK * BLK),
     )(slope, block_user, lengths, event_bucket, queries, keys, values, out_grad)
+    return pl.pallas_call(
+        hand_over,
+        out_shape=(wide,) * 4,
+        in_specs=[hbm] * 4,
+        out_specs=(hbm,) * 4,
+        scratch_shapes=[pltpu.VMEM((8, BLK // 2, RING * HD), bf16), dma((8,)), dma((8,))],
+        compiler_params=pltpu.CompilerParams(vmem_limit_bytes=62 * 2**20),
+    )(*results)
 
 
 def solution(mesh):

time: 81.3 us -> 67.6 us (0.83)
  local copies, waits for them, and re-layouts: 9.97 us -> 0 us
  Pallas kernels: 69.3 us -> 65.7 us
    unnamed x20 -> x0, local copies, waits for them, and re-layouts: 9.97 us -> none
    pallas_call x1, Pallas kernels: 69.3 us -> 63.3 us  [per_device(): pl.pallas_call(functools.partial(kernel, seqs), out_shape=(wide,) * 4, in...]
    pallas_call x0 -> x1, Pallas kernels: none -> 2.4 us  [per_device(): pl.pallas_call(hand_over, out_shape=(wide,) * 4, in_specs=[hbm] * 4, out_...]
where the time goes in v2:
time: 67.6 us; the launch traced here: 66.4 us
  Pallas kernels  65.7 us (97%)
    pallas_call x1, Pallas kernels, per_device(): pl.pallas_call(functools.partial(kernel, seqs), out_shape=(wide,) * 4, in...  63.3 us
    pallas_call x1, Pallas kernels, per_device(): pl.pallas_call(hand_over, out_shape=(wide,) * 4, in_specs=[hbm] * 4, out_...  2.4 us

profile of v2, /device:TPU:0, one launch (start us, length us, event | category | flops | bytes accessed | tf_op | source)
XLA Modules:
  0.0 66.4 jit_solution(6040700161774367047)
XLA Ops:
  0.6 63.3 %shard_map.111 = (bf16[256,1024]{1,0:T(8,128)(2,1)}, bf16[256,1024]{1,0:T(8,128)(2,1)}, bf16[256,1024]{1,0:T(8,128)(2,1)}, bf16[256,1024]{1,0:T(8,128)(2,1)}) custom-call(f32[8]{0:T(128)} %slope_hbm.1, s32[128]{0:T(128)} %user_hbm.1, s32[32]{0:T(128)} %length_hbm.1, s32[256]{0:T(256)} %bucket_hbm.1, bf16[256,1024]{1,0:T(8,128)(2,1)} %q_hbm.1, ...), custom_call_target="tpu_custom_call" | custom-call | flops 3623878656 | bytes 4194304 | tf_op jit(solution)/shard_map/pallas_call | solution.py:527
  64.0 2.4 %shard_map.112 = (bf16[256,1024]{1,0:T(8,128)(2,1)}, bf16[256,1024]{1,0:T(8,128)(2,1)}, bf16[256,1024]{1,0:T(8,128)(2,1)}, bf16[256,1024]{1,0:T(8,128)(2,1)}) custom-call(bf16[256,1024]{1,0:T(8,128)(2,1)} %get-tuple-element.8.refs_0_, bf16[256,1024]{1,0:T(8,128)(2,1)} %get-tuple-element.9.refs_1_, bf16[256,1024]{1,0:T(8,128)(2,1)} %get-tuple-element.10.refs_2_, ...), custom_call_target="tpu_custom_call" | custom-call | tf_op jit(solution)/shard_map/pallas_call | solution.py:560

commit v3 on v2

--- a/solution.py
+++ b/solution.py
@@ -10,7 +10,6 @@
 BLK = 256
 HD = 128
 RING = 8
-WHOLE = 5
 MESH = pl.DeviceIdType.MESH
 f32, bf16, i32 = jnp.float32, jnp.bfloat16, jnp.int32
 SCALE = HD ** -0.5
@@ -139,17 +138,27 @@
     self_bucket.start()
 
     def send_order(first, second):
-        def send(*tensors):
-            def body(k, _):
-                for t in tensors:
-                    in_copy(t, k).start()
-                return 0
-
-            return body
-
-        lax.fori_loop(1, WHOLE + 1, send(*first, *second), 0)
-        lax.fori_loop(WHOLE + 1, RING, send(*first), 0)
-        lax.fori_loop(WHOLE + 1, RING, send(*second), 0)
+        def send(k, tensors):
+            for t in tensors:
+                in_copy(t, k).start()
+
+        send(1, first + second)
+
+        def near(target, tensors):
+            k = 2 + 2 * ((target + core) % 2)
+            send(k, tensors)
+            send(k + 1, tensors)
+
+        def far(target, tensors):
+            send(6 + (target + core) % 2, tensors)
+
+        near(0, first + second)
+        far(0, first)
+        near(1, first)
+        far(1, first)
+        far(0, second)
+        near(1, second)
+        far(1, second)
 
     def send_buckets(k, _):
         bucket_copy(k).start()
@@ -251,57 +260,94 @@
                 copy.wait_recv()
             rowB[p + 8] = B_cross[p] * half_slope
 
-    def tile(xj, yj, xi, yi, column, row, weight, mask=None):
-        gap = jnp.abs(jnp.concatenate([column, column], axis=1) - row)
-        half = dot(xj, xi, NT) * (0.5 * SCALE) - gap
+    def products(xj, yj, xi, yi):
+        return dot(xj, xi, NT), dot(yj, yi, NT)
+
+    def pointwise(raw, d_attn, column, row, weight, mask=None):
+        half = raw * (0.5 * SCALE) - jnp.abs(jnp.concatenate([column, column], axis=1) - row)
         th = jnp.tanh(half)
         pw = th * weight + weight
         if mask is not None:
             pw = jnp.where(mask, pw, 0.0)
         aw = half * pw
-        attn = aw.astype(bf16)
-        bend = pw + aw * (1.0 - th)
-        score = (dot(yj, yi, NT) * bend).astype(bf16)
-        return (dot(attn, yi), dot(score, xi), dot(yj.T, attn), dot(xj.T, score))
-
-    def diagonal(p):
-        mask = lax.broadcasted_iota(i32, (BLK, BLK), 0) >= lax.broadcasted_iota(i32, (BLK, BLK), 1)
-        uj, wj, ui, wi = tile(QB[p], GB[p], KB[p], VB[p], colB[p], rowB[p][0:1], inv[p][0:1], mask)
-        OJ[p] += uj
-        QJ[p] += wj
-        VI[p] += ui
-        KI[p] += wi
-
-    def slot(p, r):
-        j, i = jnp.maximum(p, r), jnp.minimum(p, r)
-        upper = j >= 4
-        ja = jnp.where(upper, j + 4, j)
-        ia = jnp.where(upper, i, i + 8)
-        base = RING * seq
-        user_i, user_j = block_user(base + i), block_user(base + j)
-        inside = user_i == user_j
-        below = (block_user(base + j - 8) == user_i) & (seq > 0)
-        above = (block_user(base + i + 8) == user_j) & (seq < seqs - 1)
-        flag = jnp.where(upper, below, above)
-        valid = jnp.where(inside | flag, 1.0, 0.0)
-        on = jnp.where(flag, 1.0, 0.0)
-        off = 1.0 - on
-        weight = inv[jnp.where(upper, i, j)][0:1] * valid
-
-        def pick(a, b):
-            return lax.select(flag, a, b)
-
-        uj, wj, ui, wi = tile(
-            pick(KB[ja], QB[j]), pick(VB[ja], GB[j]), pick(QB[ia], KB[i]), pick(GB[ia], VB[i]),
-            pick(colB[ja], colB[j]), pick(rowB[ia], rowB[i])[0:1], weight)
-        OJ[j] += uj * off
-        QJ[j] += wj * off
-        FJU[j] += uj * on
-        FJW[j] += wj * on
-        VI[i] += ui * off
-        KI[i] += wi * off
-        FIU[ia] += ui * on
-        FIW[ia] += wi * on
+        return aw.astype(bf16), (d_attn * (pw + aw * (1.0 - th))).astype(bf16)
+
+    def spread(xj, yj, xi, yi, attn, score):
+        return dot(attn, yi), dot(score, xi), dot(yj.T, attn), dot(xj.T, score)
+
+    class Diagonal:
+        def __init__(self, p):
+            self.p = p
+            self.operands = (QB[p], GB[p], KB[p], VB[p])
+
+        def first(self):
+            self.raw = products(*self.operands)
+
+        def second(self):
+            p = self.p
+            mask = lax.broadcasted_iota(i32, (BLK, BLK), 0) >= lax.broadcasted_iota(i32, (BLK, BLK), 1)
+            self.tiles = pointwise(*self.raw, colB[p], rowB[p][0:1], inv[p][0:1], mask)
+
+        def third(self):
+            p = self.p
+            uj, wj, ui, wi = spread(*self.operands, *self.tiles)
+            OJ[p] += uj
+            QJ[p] += wj
+            VI[p] += ui
+            KI[p] += wi
+
+    class Slot:
+        def __init__(self, p, r):
+            j, i = jnp.maximum(p, r), jnp.minimum(p, r)
+            upper = j >= 4
+            ja = jnp.where(upper, j + 4, j)
+            ia = jnp.where(upper, i, i + 8)
+            base = RING * seq
+            user_i, user_j = block_user(base + i), block_user(base + j)
+            inside = user_i == user_j
+            below = (block_user(base + j - 8) == user_i) & (seq > 0)
+            above = (block_user(base + i + 8) == user_j) & (seq < seqs - 1)
+            flag = jnp.where(upper, below, above)
+            valid = jnp.where(inside | flag, 1.0, 0.0)
+            self.on = jnp.where(flag, 1.0, 0.0)
+            self.weight = inv[jnp.where(upper, i, j)][0:1] * valid
+            self.where = (j, i, ja, ia)
+
+            def pick(a, b):
+                return lax.select(flag, a, b)
+
+            self.pick = pick
+            self.operands = (pick(KB[ja], QB[j]), pick(VB[ja], GB[j]), pick(QB[ia], KB[i]), pick(GB[ia], VB[i]))
+
+        def first(self):
+            self.raw = products(*self.operands)
+
+        def second(self):
+            j, i, ja, ia = self.where
+            self.tiles = pointwise(
+                *self.raw, self.pick(colB[ja], colB[j]), self.pick(rowB[ia], rowB[i])[0:1], self.weight)
+
+        def third(self):
+            j, i, ja, ia = self.where
+            on, off = self.on, 1.0 - self.on
+            uj, wj, ui, wi = spread(*self.operands, *self.tiles)
+            OJ[j] += uj * off
+            QJ[j] += wj * off
+            FJU[j] += uj * on
+            FJW[j] += wj * on
+            VI[i] += ui * off
+            KI[i] += wi * off
+            FIU[ia] += ui * on
+            FIW[ia] += wi * on
+
+    def together(*pairs):
+        for pair_ in pairs:
+            pair_.first()
+        pairs[0].second()
+        for n, pair_ in enumerate(pairs):
+            if n + 1 < len(pairs):
+                pairs[n + 1].second()
+            pair_.third()
 
     back = 0.5 * SCALE
 
@@ -377,27 +423,24 @@
         p = source(k)
 
         def two(m, _):
-            slot(p, source(2 * m))
-            slot(p, source(2 * m + 1))
+            together(Slot(p, source(2 * m)), Slot(p, source(2 * m + 1)))
             return 0
 
         lax.fori_loop(0, k // 2, two, 0)
 
         @pl.when(k % 2 == 1)
         def _():
-            slot(p, source(k - 1))
-            diagonal(p)
+            together(Slot(p, source(k - 1)), Diagonal(p))
 
         @pl.when(k % 2 == 0)
         def _():
-            diagonal(p)
+            together(Diagonal(p))
 
         return 0
 
     def advance(k, _):
-        first = jnp.where(k == 0, 0, jnp.where(k < 4, 4, jnp.where(k < 6, k, 7)))
-        first = jnp.where(k == 5, 6, first)
-        end = jnp.where(k < 4, 4, jnp.where(k == 4, 6, jnp.where(k == 5, 7, 8)))
+        first = jnp.where(k == 0, 0, jnp.where(k == 2, 2, 6))
+        end = jnp.where(k == 0, 2, jnp.where(k == 2, 6 + 2 * core, jnp.where(k == 4, 8 - 2 * core, 6)))
         lax.fori_loop(first, end, pass_on, 0)
         step(k, 0)
         return 0
@@ -411,15 +454,13 @@
 
     def last_two(m, _):
         one, two = turn(2 * m), turn(2 * m + 1)
-        slot(last, one)
-        slot(last, two)
+        together(Slot(last, one), Slot(last, two))
         finish(one)
         finish(two)
         return 0
 
     lax.fori_loop(0, 3, last_two, 0)
-    slot(last, turn(6))
-    diagonal(last)
+    together(Slot(last, turn(6)), Diagonal(last))
     finish(last)
     finish(turn(6))
 
@@ -444,7 +485,6 @@
 
         return 0
 
-    lax.fori_loop(0, RING, drain_in, 0)
 
     def settle(k, _):
         p = source((k + 2) % RING)
@@ -470,6 +510,7 @@
         return 0
 
     lax.fori_loop(0, RING, settle, 0)
+    lax.fori_loop(0, RING, drain_in, 0)
 
     def drain_out(k, _):
         p = source(k)

time: 67.6 us -> 65.5 us (0.969); the launches traced: 66.4 us -> 65.3 us
  Pallas kernels: 65.7 us -> 64.6 us
    pallas_call x1, Pallas kernels: 63.3 us -> 62.2 us  [per_device(): pl.pallas_call(functools.partial(kernel, seqs), out_shape=(wide,) * 4, in...]
where the time goes in v3:
time: 65.5 us; the launch traced here: 65.3 us
  Pallas kernels  64.6 us (99%)
    pallas_call x1, Pallas kernels, per_device(): pl.pallas_call(functools.partial(kernel, seqs), out_shape=(wide,) * 4, in...  62.2 us
    pallas_call x1, Pallas kernels, per_device(): pl.pallas_call(hand_over, out_shape=(wide,) * 4, in_specs=[hbm] * 4, out_...  2.4 us

profile of v3, /device:TPU:0, one launch (start us, length us, event | category | flops | bytes accessed | tf_op | source)
XLA Modules:
  0.0 65.3 jit_solution(13937761133258990167)
XLA Ops:
  0.6 62.2 %shard_map.111 = (bf16[256,1024]{1,0:T(8,128)(2,1)}, bf16[256,1024]{1,0:T(8,128)(2,1)}, bf16[256,1024]{1,0:T(8,128)(2,1)}, bf16[256,1024]{1,0:T(8,128)(2,1)}) custom-call(f32[8]{0:T(128)} %slope_hbm.1, s32[128]{0:T(128)} %user_hbm.1, s32[32]{0:T(128)} %length_hbm.1, s32[256]{0:T(256)} %bucket_hbm.1, bf16[256,1024]{1,0:T(8,128)(2,1)} %q_hbm.1, ...), custom_call_target="tpu_custom_call" | custom-call | flops 3623878656 | bytes 4194304 | tf_op jit(solution)/shard_map/pallas_call | solution.py:568
  62.9 2.4 %shard_map.112 = (bf16[256,1024]{1,0:T(8,128)(2,1)}, bf16[256,1024]{1,0:T(8,128)(2,1)}, bf16[256,1024]{1,0:T(8,128)(2,1)}, bf16[256,1024]{1,0:T(8,128)(2,1)}) custom-call(bf16[256,1024]{1,0:T(8,128)(2,1)} %get-tuple-element.8.refs_0_, bf16[256,1024]{1,0:T(8,128)(2,1)} %get-tuple-element.9.refs_1_, bf16[256,1024]{1,0:T(8,128)(2,1)} %get-tuple-element.10.refs_2_, ...), custom_call_target="tpu_custom_call" | custom-call | tf_op jit(solution)/shard_map/pallas_call | solution.py:601

commit v4 on v3

--- a/solution.py
+++ b/solution.py
@@ -33,6 +33,7 @@
     blocks = seqs * RING
     y, core = pair // 2, pair % 2
     up, down = (seq + 1) % seqs, (seq + seqs - 1) % seqs
+    has_up, has_down = seq < seqs - 1, seq > 0
     outs = (o_out, dq_out, dk_out, dv_out)
     rings = (QB, KB, VB, GB)
 
@@ -56,8 +57,15 @@
         return 0
 
     lax.fori_loop(1, RING, greet, 0)
-    pl.semaphore_signal(barrier, inc=1, device_id=(up, pair), device_id_type=MESH)
-    pl.semaphore_signal(barrier, inc=1, device_id=(down, pair), device_id_type=MESH)
+
+    @pl.when(has_up)
+    def _():
+        pl.semaphore_signal(barrier, inc=1, device_id=(up, pair), device_id_type=MESH)
+
+    @pl.when(has_down)
+    def _():
+        pl.semaphore_signal(barrier, inc=1, device_id=(down, pair), device_id_type=MESH)
+
 
     load = pltpu.make_async_copy(g_hbm, G_own, load_sem)
     load.start()
@@ -96,6 +104,28 @@
             FIU[8 + p] = zero
             FIW[8 + p] = zero
 
+        @pl.when((p >= 4) & (seq == 0))
+        def _():
+            KB[p + 4] = jnp.zeros((BLK, HD), bf16)
+            VB[p + 4] = jnp.zeros((BLK, HD), bf16)
+            colB[p + 4] = jnp.zeros((BLK, HD), f32)
+
+        @pl.when((p < 3) & (seq == 0))
+        def _():
+            cross_in[0, p] = jnp.zeros((BLK, HD), bf16)
+            cross_in[1, p] = jnp.zeros((BLK, HD), bf16)
+
+        @pl.when((p < 3) & (seq == seqs - 1))
+        def _():
+            QB[p + 8] = jnp.zeros((BLK, HD), bf16)
+            GB[p + 8] = jnp.zeros((BLK, HD), bf16)
+            rowB[p + 8] = jnp.zeros((8, BLK), f32)
+
+        @pl.when((p >= 4) & (seq == seqs - 1))
+        def _():
+            cross_in[0, p] = jnp.zeros((BLK, HD), bf16)
+            cross_in[1, p] = jnp.zeros((BLK, HD), bf16)
+
         length = length_ref[block_user(RING * seq + p)]
         inv[p] = 1.0 / jnp.full((8, BLK), length.astype(f32), f32)
         return 0
@@ -112,7 +142,7 @@
         return 0
 
     lax.fori_loop(0, BLK // 32, mask_own, 0)
-    pl.semaphore_wait(barrier, RING + 1)
+    pl.semaphore_wait(barrier, RING - 1 + jnp.where(has_up, 1, 0) + jnp.where(has_down, 1, 0))
 
     sources = (q_hbm, k_hbm, v_hbm, G_own)
 
@@ -208,8 +238,10 @@
                 wait_in(1, p)
                 wait_in(2, p)
 
-            for copy in cross_copies(p, True):
-                copy.start()
+            @pl.when(has_up)
+            def _():
+                for copy in cross_copies(p, True):
+                    copy.start()
 
         @pl.when(p < 4)
         def _():
@@ -218,7 +250,7 @@
                 wait_in(0, p)
                 wait_in(3, p)
 
-            @pl.when(p < 3)
+            @pl.when((p < 3) & has_down)
             def _():
                 for copy in cross_copies(p, False):
                     copy.start()
@@ -247,14 +279,14 @@
         rowB[p] = row
         colB[p] = jnp.broadcast_to(row[0:1], (HD, BLK)).T
 
-        @pl.when(p >= 4)
+        @pl.when((p >= 4) & has_down)
         def _():
             for copy in cross_copies(p, True):
                 copy.wait_recv()
             crossed = B_cross[p] * half_slope
             colB[p + 4] = jnp.broadcast_to(crossed[0:1], (HD, BLK)).T
 
-        @pl.when(p < 3)
+        @pl.when((p < 3) & has_up)
         def _():
             for copy in cross_copies(p, False):
                 copy.wait_recv()
@@ -340,14 +372,16 @@
             FIU[ia] += ui * on
             FIW[ia] += wi * on
 
-    def together(*pairs):
-        for pair_ in pairs:
-            pair_.first()
-        pairs[0].second()
-        for n, pair_ in enumerate(pairs):
-            if n + 1 < len(pairs):
-                pairs[n + 1].second()
-            pair_.third()
+    def together(*tiles):
+        count = len(tiles)
+        tiles[0].first()
+        for n in range(count + 1):
+            if n + 1 < count:
+                tiles[n + 1].first()
+            if n < count:
+                tiles[n].second()
+            if n >= 1:
+                tiles[n - 1].third()
 
     back = 0.5 * SCALE
 
@@ -390,8 +424,12 @@
         def _():
             cross_out[0, p] = FJU[p].astype(bf16)
             cross_out[1, p] = (FJW[p] * back).astype(bf16)
-            for copy in return_copies(p, True):
-                copy.start()
+
+            @pl.when(has_down)
+            def _():
+                for copy in return_copies(p, True):
+                    copy.start()
+
             FJU[p] = dv
             FJW[p] = dk
 
@@ -399,8 +437,12 @@
         def _():
             cross_out[0, p] = FIU[p + 8].T.astype(bf16)
             cross_out[1, p] = (FIW[p + 8].T * back).astype(bf16)
-            for copy in return_copies(p, False):
-                copy.start()
+
+            @pl.when(has_up)
+            def _():
+                for copy in return_copies(p, False):
+                    copy.start()
+
             OJ[p] = o
             QJ[p] = dq
 
@@ -422,19 +464,28 @@
         arrive(k)
         p = source(k)
 
-        def two(m, _):
-            together(Slot(p, source(2 * m)), Slot(p, source(2 * m + 1)))
+        def four(m, _):
+            together(*[Slot(p, source(4 * m + n)) for n in range(4)])
             return 0
 
-        lax.fori_loop(0, k // 2, two, 0)
-
-        @pl.when(k % 2 == 1)
-        def _():
-            together(Slot(p, source(k - 1)), Diagonal(p))
-
-        @pl.when(k % 2 == 0)
+        lax.fori_loop(0, k // 4, four, 0)
+        rest = k - k % 4
+
+        @pl.when(k % 4 == 0)
         def _():
             together(Diagonal(p))
+
+        @pl.when(k % 4 == 1)
+        def _():
+            together(Slot(p, source(rest)), Diagonal(p))
+
+        @pl.when(k % 4 == 2)
+        def _():
+            together(Slot(p, source(rest)), Slot(p, source(rest + 1)), Diagonal(p))
+
+        @pl.when(k % 4 == 3)
+        def _():
+            together(*[Slot(p, source(rest + n)) for n in range(3)], Diagonal(p))
 
         return 0
 
@@ -467,12 +518,12 @@
     def drain_in(k, _):
         p = source(k)
 
-        @pl.when(p >= 4)
+        @pl.when((p >= 4) & has_up)
         def _():
             for copy in cross_copies(p, True):
                 copy.wait_send()
 
-        @pl.when(p < 3)
+        @pl.when((p < 3) & has_down)
         def _():
             for copy in cross_copies(p, False):
                 copy.wait_send()
@@ -491,8 +542,11 @@
 
         @pl.when(p >= 4)
         def _():
-            for copy in return_copies(p, True):
-                copy.wait_recv()
+            @pl.when(has_up)
+            def _():
+                for copy in return_copies(p, True):
+                    copy.wait_recv()
+
             stage[2, p] = (FJW[p] + cross_in[1, p].astype(f32)).astype(bf16)
             stage[3, p] = (FJU[p] + cross_in[0, p].astype(f32)).astype(bf16)
             emit(2, p)
@@ -500,8 +554,11 @@
 
         @pl.when(p < 3)
         def _():
-            for copy in return_copies(p, False):
-                copy.wait_recv()
+            @pl.when(has_down)
+            def _():
+                for copy in return_copies(p, False):
+                    copy.wait_recv()
+
             stage[0, p] = jnp.where(live_mask(p), OJ[p] + cross_in[0, p].astype(f32), 0.0).astype(bf16)
             stage[1, p] = (QJ[p] + cross_in[1, p].astype(f32)).astype(bf16)
             emit(0, p)
@@ -515,12 +572,12 @@
     def drain_out(k, _):
         p = source(k)
 
-        @pl.when(p >= 4)
+        @pl.when((p >= 4) & has_down)
         def _():
             for copy in return_copies(p, True):
                 copy.wait_send()
 
-        @pl.when(p < 3)
+        @pl.when((p < 3) & has_up)
         def _():
             for copy in return_copies(p, False):
                 copy.wait_send()

time: 65.5 us -> 62.2 us (0.950)
  the two profiles are of different devices: /device:TPU:0 before, /device:TPU:68 now
where the time goes in v4:
time: 62.2 us; the launch traced here: 62 us
  Pallas kernels  61.3 us (99%)
  between operations  0.64 us (1%)
    pallas_call x1, Pallas kernels, per_device(): pl.pallas_call(functools.partial(kernel, seqs), out_shape=(wide,) * 4, in...  58.9 us
    pallas_call x1, Pallas kernels, per_device(): pl.pallas_call(hand_over, out_shape=(wide,) * 4, in_specs=[hbm] * 4, out_...  2.4 us

profile of v4, /device:TPU:68, one launch (start us, length us, event | category | flops | bytes accessed | tf_op | source)
XLA Modules:
  0.0 62.0 jit_solution(13852210723643341379)
XLA Ops:
  0.6 58.9 %shard_map.111 = (bf16[256,1024]{1,0:T(8,128)(2,1)}, bf16[256,1024]{1,0:T(8,128)(2,1)}, bf16[256,1024]{1,0:T(8,128)(2,1)}, bf16[256,1024]{1,0:T(8,128)(2,1)}) custom-call(f32[8]{0:T(128)} %slope_hbm.1, s32[128]{0:T(128)} %user_hbm.1, s32[32]{0:T(128)} %length_hbm.1, s32[256]{0:T(256)} %bucket_hbm.1, bf16[256,1024]{1,0:T(8,128)(2,1)} %q_hbm.1, ...), custom_call_target="tpu_custom_call" | custom-call | flops 3623878656 | bytes 4194304 | tf_op jit(solution)/shard_map/pallas_call | solution.py:625
  59.6 2.4 %shard_map.112 = (bf16[256,1024]{1,0:T(8,128)(2,1)}, bf16[256,1024]{1,0:T(8,128)(2,1)}, bf16[256,1024]{1,0:T(8,128)(2,1)}, bf16[256,1024]{1,0:T(8,128)(2,1)}) custom-call(bf16[256,1024]{1,0:T(8,128)(2,1)} %get-tuple-element.8.refs_0_, bf16[256,1024]{1,0:T(8,128)(2,1)} %get-tuple-element.9.refs_1_, bf16[256,1024]{1,0:T(8,128)(2,1)} %get-tuple-element.10.refs_2_, ...), custom_call_target="tpu_custom_call" | custom-call | tf_op jit(solution)/shard_map/pallas_call | solution.py:658

commit v5 on v4

--- a/solution.py
+++ b/solution.py
@@ -185,8 +185,8 @@
         near(0, first + second)
         far(0, first)
         near(1, first)
+        far(0, second)
         far(1, first)
-        far(0, second)
         near(1, second)
         far(1, second)
 
@@ -415,10 +415,19 @@
         return lax.broadcasted_iota(i32, (BLK, HD), 0) < live_rows(RING * seq + p)
 
     def finish(p):
-        o = OJ[p] + FIU[p].T
-        dq = (QJ[p] + FIW[p].T) * back
-        dv = VI[p].T
-        dk = KI[p].T * back
+        @pl.when(p >= 3)
+        def _():
+            stage[0, p] = jnp.where(live_mask(p), OJ[p] + FIU[p].T, 0.0).astype(bf16)
+            emit(0, p)
+            stage[1, p] = ((QJ[p] + FIW[p].T) * back).astype(bf16)
+            emit(1, p)
+
+        @pl.when(p < 4)
+        def _():
+            stage[2, p] = ((KI[p].T + FJW[p]) * back).astype(bf16)
+            emit(2, p)
+            stage[3, p] = (VI[p].T + FJU[p]).astype(bf16)
+            emit(3, p)
 
         @pl.when(p >= 4)
         def _():
@@ -430,8 +439,8 @@
                 for copy in return_copies(p, True):
                     copy.start()
 
-            FJU[p] = dv
-            FJW[p] = dk
+            FJU[p] = VI[p].T
+            FJW[p] = KI[p].T * back
 
         @pl.when(p < 3)
         def _():
@@ -443,22 +452,8 @@
                 for copy in return_copies(p, False):
                     copy.start()
 
-            OJ[p] = o
-            QJ[p] = dq
-
-        @pl.when(p >= 3)
-        def _():
-            stage[0, p] = jnp.where(live_mask(p), o, 0.0).astype(bf16)
-            stage[1, p] = dq.astype(bf16)
-            emit(0, p)
-            emit(1, p)
-
-        @pl.when(p < 4)
-        def _():
-            stage[2, p] = (dk + FJW[p] * back).astype(bf16)
-            stage[3, p] = (dv + FJU[p]).astype(bf16)
-            emit(2, p)
-            emit(3, p)
+            OJ[p] = OJ[p] + FIU[p].T
+            QJ[p] = (QJ[p] + FIW[p].T) * back
 
     def step(k, _):
         arrive(k)
@@ -491,7 +486,7 @@
 
     def advance(k, _):
         first = jnp.where(k == 0, 0, jnp.where(k == 2, 2, 6))
-        end = jnp.where(k == 0, 2, jnp.where(k == 2, 6 + 2 * core, jnp.where(k == 4, 8 - 2 * core, 6)))
+        end = jnp.where(k == 0, 2, jnp.where(k == 2, 6, jnp.where(k == 4, 8, 6)))
         lax.fori_loop(first, end, pass_on, 0)
         step(k, 0)
         return 0

time: 62.2 us -> 61.2 us (0.984)
  the two profiles are of different devices: /device:TPU:68 before, /device:TPU:0 now
where the time goes in v5:
time: 61.2 us; the launch traced here: 60.7 us
  Pallas kernels  60.1 us (98%)
  between operations  0.64 us (1%)
    pallas_call x1, Pallas kernels, per_device(): pl.pallas_call(functools.partial(kernel, seqs), out_shape=(wide,) * 4, in...  57.7 us
    pallas_call x1, Pallas kernels, per_device(): pl.pallas_call(hand_over, out_shape=(wide,) * 4, in_specs=[hbm] * 4, out_...  2.4 us

profile of v5, /device:TPU:0, one launch (start us, length us, event | category | flops | bytes accessed | tf_op | source)
XLA Modules:
  0.0 60.7 jit_solution(8780379871651679750)
XLA Ops:
  0.6 57.7 %shard_map.111 = (bf16[256,1024]{1,0:T(8,128)(2,1)}, bf16[256,1024]{1,0:T(8,128)(2,1)}, bf16[256,1024]{1,0:T(8,128)(2,1)}, bf16[256,1024]{1,0:T(8,128)(2,1)}) custom-call(f32[8]{0:T(128)} %slope_hbm.1, s32[128]{0:T(128)} %user_hbm.1, s32[32]{0:T(128)} %length_hbm.1, s32[256]{0:T(256)} %bucket_hbm.1, bf16[256,1024]{1,0:T(8,128)(2,1)} %q_hbm.1, ...), custom_call_target="tpu_custom_call" | custom-call | flops 3623878656 | bytes 4194304 | tf_op jit(solution)/shard_map/pallas_call | solution.py:620
  58.3 2.4 %shard_map.112 = (bf16[256,1024]{1,0:T(8,128)(2,1)}, bf16[256,1024]{1,0:T(8,128)(2,1)}, bf16[256,1024]{1,0:T(8,128)(2,1)}, bf16[256,1024]{1,0:T(8,128)(2,1)}) custom-call(bf16[256,1024]{1,0:T(8,128)(2,1)} %get-tuple-element.8.refs_0_, bf16[256,1024]{1,0:T(8,128)(2,1)} %get-tuple-element.9.refs_1_, bf16[256,1024]{1,0:T(8,128)(2,1)} %get-tuple-element.10.refs_2_, ...), custom_call_target="tpu_custom_call" | custom-call | tf_op jit(solution)/shard_map/pallas_call | solution.py:653

commit v6 on v5

--- a/solution.py
+++ b/solution.py
@@ -182,7 +182,8 @@
         def far(target, tensors):
             send(6 + (target + core) % 2, tensors)
 
-        near(0, first + second)
+        near(0, first)
+        near(0, second)
         far(0, first)
         near(1, first)
         far(0, second)
@@ -224,6 +225,8 @@
             for n, (src, dst) in enumerate(pairs)
         ]
 
+    half_slope = 0.5 * slope_ref[pair]
+
     def pass_on(k, _):
         p = source(k)
 
@@ -254,30 +257,28 @@
             def _():
                 for copy in cross_copies(p, False):
                     copy.start()
-
-        return 0
-
-
-    half_slope = 0.5 * slope_ref[pair]
-
-    def arrive(k):
-        p = source(k)
-
-        @pl.when(k > 0)
-        def _():
-            @pl.when(p >= 4)
-            def _():
-                wait_in(0, p)
-                wait_in(3, p)
-
-            @pl.when(p < 4)
-            def _():
-                wait_in(1, p)
-                wait_in(2, p)
 
         row = B_ring[p] * half_slope
         rowB[p] = row
         colB[p] = jnp.broadcast_to(row[0:1], (HD, BLK)).T
+        return 0
+
+
+    def arrive(k):
+        p = source(k)
+
+        @pl.when(k > 0)
+        def _():
+            @pl.when(p >= 4)
+            def _():
+                wait_in(0, p)
+                wait_in(3, p)
+
+            @pl.when(p < 4)
+            def _():
+                wait_in(1, p)
+                wait_in(2, p)
+
 
         @pl.when((p >= 4) & has_down)
         def _():

time: 61.2 us -> 60.9 us (level)
  no operation moved by 1% of the time
where the time goes in v6:
time: 60.9 us; the launch traced here: 60.4 us
  Pallas kernels  59.8 us (98%)
  between operations  0.64 us (1%)
    pallas_call x1, Pallas kernels, per_device(): pl.pallas_call(functools.partial(kernel, seqs), out_shape=(wide,) * 4, in...  57.4 us
    pallas_call x1, Pallas kernels, per_device(): pl.pallas_call(hand_over, out_shape=(wide,) * 4, in_specs=[hbm] * 4, out_...  2.4 us

profile of v6, /device:TPU:0, one launch (start us, length us, event | category | flops | bytes accessed | tf_op | source)
XLA Modules:
  0.0 60.4 jit_solution(12132885572573270011)
XLA Ops:
  0.6 57.4 %shard_map.111 = (bf16[256,1024]{1,0:T(8,128)(2,1)}, bf16[256,1024]{1,0:T(8,128)(2,1)}, bf16[256,1024]{1,0:T(8,128)(2,1)}, bf16[256,1024]{1,0:T(8,128)(2,1)}) custom-call(f32[8]{0:T(128)} %slope_hbm.1, s32[128]{0:T(128)} %user_hbm.1, s32[32]{0:T(128)} %length_hbm.1, s32[256]{0:T(256)} %bucket_hbm.1, bf16[256,1024]{1,0:T(8,128)(2,1)} %q_hbm.1, ...), custom_call_target="tpu_custom_call" | custom-call | flops 3623878656 | bytes 4194304 | tf_op jit(solution)/shard_map/pallas_call | solution.py:621
  58.0 2.4 %shard_map.112 = (bf16[256,1024]{1,0:T(8,128)(2,1)}, bf16[256,1024]{1,0:T(8,128)(2,1)}, bf16[256,1024]{1,0:T(8,128)(2,1)}, bf16[256,1024]{1,0:T(8,128)(2,1)}) custom-call(bf16[256,1024]{1,0:T(8,128)(2,1)} %get-tuple-element.8.refs_0_, bf16[256,1024]{1,0:T(8,128)(2,1)} %get-tuple-element.9.refs_1_, bf16[256,1024]{1,0:T(8,128)(2,1)} %get-tuple-element.10.refs_2_, ...), custom_call_target="tpu_custom_call" | custom-call | tf_op jit(solution)/shard_map/pallas_call | solution.py:654
